TPU v7x, 128 devices: a whole 4x4x4 slice. The times are simulated.
128 devices in a mesh: row: 8 (over z, core), col: 16 (over x, y).
Axes of the slice: x: 4, y: 4, z: 4, core: 2. Of those that a mesh axis runs over, the one named last changes fastest.
Arguments:
- amplitudes: float32 [16, 160, 256, 256], P('row', None, 'col'), may hold values from -6 to 6
- integrals: float32 [160, 256, 2560], P('row', 'col'), may hold values from -0.03125 to 0.03125
- occ_irrep: int32 [150], replicated, may hold values from 0 to 7, as said below
- vir_irrep: int32 [1500], replicated, may hold values from 0 to 7, as said below
Outputs:
- cycle_term: float32 [16, 256, 2560], P('row', 'col')
Inputs may be any that keep to these rules, and one draw needn't show every extreme that they name: `occ_irrep`: nondecreasing. `vir_irrep`: nondecreasing; no label is carried by more than 256 virtual orbitals, and some label is carried by exactly 256.
All inputs are finite; a program needn't handle non-finite values.
Results may differ from a plain program's by a relative error of at most 0.00007.
Values sent between devices are 32-bit elements; how exact they have to be, the bound alone decides.
No kernel may reach another device: no remote copies, remote signals or barrier semaphores. Data moves between devices by JAX's collectives and lax.ppermute only.
A program may use at most 192 MiB of HBM per device.

v0:
```python
import jax
import jax.numpy as jnp
from jax import lax
from jax.sharding import PartitionSpec as P


def irrep_counts(vir_irrep):
    labels = jnp.arange(8, dtype=jnp.int32)
    return jnp.sum((vir_irrep[:, None] == labels[None, :]).astype(jnp.int32), axis=0)


def block_sizes(orbital_irreps, counts):
    labels = jnp.arange(8, dtype=jnp.int32)
    return jnp.sum(
        jnp.where(orbital_irreps[:, None] == labels[None, :], counts[None, :], 0), axis=1
    )


def slot_mask(padded, counts, occupied, slot_start, slot_count, virtual_count):
    slot_index = slot_start + jnp.arange(slot_count, dtype=jnp.int32)
    irreps_here = lax.dynamic_slice_in_dim(padded, slot_start, slot_count)
    block_size = jnp.where(slot_index < occupied, block_sizes(irreps_here, counts), 0)
    virtual_index = jnp.arange(virtual_count, dtype=jnp.int32)
    return (virtual_index[None, :] < block_size[:, None]).astype(jnp.float32)


def body(amplitudes, integrals, occ_irrep, vir_irrep):
    row_count = lax.axis_size("row")
    row_index = lax.axis_index("row")
    col_index = lax.axis_index("col")
    local_orbitals, slot_total, local_virtual, virtual_cap = amplitudes.shape
    local_slots, local_columns, panel_width = integrals.shape
    occupied = occ_irrep.shape[0]
    window_total = local_orbitals * row_count
    counts = irrep_counts(vir_irrep)
    padded = jnp.concatenate([occ_irrep, jnp.zeros((slot_total - occupied,), jnp.int32)])
    relaid = lax.all_to_all(amplitudes, "row", split_axis=1, concat_axis=0, tiled=True)
    slot_start = row_index * local_slots
    segment = lax.all_gather(integrals, "col", axis=1, tiled=True)
    column_span = segment.shape[1]
    live_mask = slot_mask(padded, counts, occupied, slot_start, local_slots, column_span)
    partial_value = jnp.einsum(
        "ikac,kcn->ian", relaid, segment * live_mask[:, :, None], precision=lax.Precision.HIGHEST
    )
    cycle_term = lax.psum_scatter(partial_value, "row", scatter_dimension=0, tiled=True)
    window_index = row_index * local_orbitals + jnp.arange(local_orbitals, dtype=jnp.int32)
    orbital = window_index * occupied // window_total
    matches = jnp.arange(occupied, dtype=jnp.int32)[None, :] == orbital[:, None]
    window_irreps = jnp.sum(jnp.where(matches, occ_irrep[None, :], 0), axis=1)
    row_sizes = block_sizes(window_irreps, counts)
    virtual_index = col_index * local_virtual + jnp.arange(local_virtual, dtype=jnp.int32)
    rowmask = (virtual_index[None, :] < row_sizes[:, None]).astype(jnp.float32)
    return cycle_term * rowmask[:, :, None]


def solution(mesh):
    return jax.shard_map(
        body,
        mesh=mesh,
        in_specs=(P("row", None, "col", None), P("row", "col", None), P(), P()),
        out_specs=P("row", "col", None),
        check_vma=False,
    )
```

profile of v0, /device:TPU:0, one launch (start us, length us, event | category | flops | bytes accessed | tf_op | source)
XLA Modules:
  0.0 402.6 jit_solution(16216572025394648375)
XLA Ops:
  6.5 0.0 all-gather.2.cloned.1.call-start
  6.5 0.7 all-gather.2.cloned.1.call-update
  7.3 5.6 %copy.8 = f32[2,160,16,256]{3,2,0,1:T(8,128)} copy(f32[2,160,16,256]{3,2,1,0:T(8,128)} %param.4) | data formatting | bytes 10485760 | tf_op args[0]
  12.9 0.0 copy-start.1
  12.9 0.0 copy-start
  12.9 5.5 %all-to-all-start = ((f32[2,160,16,256]{3,2,0,1:T(8,128)}), f32[2,160,16,256]{3,2,0,1:T(8,128)}, u32[]{:S(2)}, u32[]{:S(2)}) async-start(f32[2,160,16,256]{3,2,0,1:T(8,128)} %copy.8), calls=%async_computation | async-start | bytes 10485760 | tf_op jit(solution)/shard_map/all_to_all | solution.py:37
  18.4 0.0 reduce-scatter.2.cloned.1.call-start
  18.5 0.0 copy-done.1
  18.5 0.1 pad_dynamic-slice_fusion
  18.6 0.0 copy-done
  18.6 0.1 convert_reduce_fusion
  18.7 0.1 select_reduce_fusion
  18.8 0.1 fusion.7
  18.9 60.6 %all-to-all-done = f32[2,160,16,256]{3,2,0,1:T(8,128)} async-done(((f32[2,160,16,256]{3,2,0,1:T(8,128)}), f32[2,160,16,256]{3,2,0,1:T(8,128)}, u32[]{:S(2)}, u32[]{:S(2)}) %all-to-all-start) | async-done | bytes 5242912 | tf_op jit(solution)/shard_map/all_to_all | solution.py:37
  79.4 5.6 %copy.9 = f32[2,8,20,16,256]{4,3,2,0,1:T(8,128)} copy(f32[2,8,20,16,256]{4,3,0,2,1:T(8,128)} %bitcast.1) | data formatting | bytes 10485760 | tf_op jit(solution)/shard_map/all_to_all | solution.py:37
  85.1 220.4 %all-gather.2.cloned.1.call-done = f32[20,256,2560]{2,1,0:T(8,128)} async-done(((f32[20,16,2560]{2,1,0:T(8,128)}), f32[20,256,2560]{2,1,0:T(8,128)}) %all-gather.2.cloned.1.call-update) | async-done | bytes 52428816 | tf_op jit(solution)/shard_map/all_gather | solution.py:39
  305.4 53.7 %fusion.4 = f32[16,16,2560]{2,1,0:T(8,128)} fusion(f32[16,20,16,256]{3,2,1,0:T(8,128)} %bitcast.19, f32[20,256,2560]{2,1,0:T(8,128)} %all-gather.2.cloned.1.call-done, f32[20,256]{1,0:T(8,128)S(1)} %fusion.7), kind=kOutput, calls=%fused_computation.4 | convolution fusion | flops 40278425600 | bytes 60313600 | tf_op jit(solution)/shard_map/ikac,kcn->ian/dot_general | solution.py:42
  359.2 0.0 reduce-scatter.2.cloned.1.call-update
  359.2 0.2 fusion.8
  359.4 0.2 fusion.9
  359.6 0.1 compare_convert_fusion
  359.7 34.3 %reduce-scatter.2.cloned.1.call-done = f32[2,16,2560]{2,1,0:T(8,128)} async-done(((f32[16,16,2560]{2,1,0:T(8,128)}), f32[2,16,2560]{2,1,0:T(8,128)}) %reduce-scatter.2.cloned.1.call-update) | async-done | bytes 327696 | tf_op jit(solution)/shard_map/reduce_scatter | solution.py:45
  394.0 1.8 broadcast_multiply_fusion
  (3 shorter events, 0.0 us)
Async XLA Ops:
  6.5 298.9 %all-gather.2.cloned.1.call-start = ((), (), s32[]{:S(2)}) async-start(), calls=%async_computation.2 | async-start | bytes 55705600 | tf_op jit(solution)/shard_map/all_gather | solution.py:39
  12.9 5.6 %copy-start.1 = (s32[150]{0:T(256)S(1)}, s32[150]{0:T(256)}, u32[]{:S(2)}) copy-start(s32[150]{0:T(256)} %param.6) | copy-start | bytes 1804
  12.9 5.7 %copy-start = (s32[1500]{0:T(1024)S(1)}, s32[1500]{0:T(1024)}, u32[]{:S(2)}) copy-start(s32[1500]{0:T(1024)} %param.7) | copy-start | bytes 18004
  12.9 66.5 %all-to-all-start = ((f32[2,160,16,256]{3,2,0,1:T(8,128)}), f32[2,160,16,256]{3,2,0,1:T(8,128)}, u32[]{:S(2)}, u32[]{:S(2)}) async-start(f32[2,160,16,256]{3,2,0,1:T(8,128)} %copy.8), calls=%async_computation | async-start | bytes 10485760 | tf_op jit(solution)/shard_map/all_to_all | solution.py:37
  18.4 375.6 %reduce-scatter.2.cloned.1.call-start = ((), (), s32[]{:S(2)}) async-start(), calls=%async_computation.3 | async-start | bytes 2949120 | tf_op jit(solution)/shard_map/reduce_scatter | solution.py:45
Sparse Core Ops, SparseCore 0:
  9.5 295.8 all-gather.1
  359.3 34.6 reduce-scatter.1
where the time goes:
time: 403 us
  waiting for transfers between devices  316 us (78%)
  matrix products  53.7 us (13%)
  between operations  13.4 us (3%)
  local copies, waits for them, and re-layouts  11.4 us (3%)
  starting transfers between devices  5.57 us (1%)
    all_gather x1, waiting for transfers between devices, body(): segment = lax.all_gather(integrals, 'col', axis=1, tiled=True)  220 us
    all_to_all x1, waiting for transfers between devices, body(): lax.all_to_all(amplitudes, 'row', split_axis=1, concat_axis=0, tiled=True)  60.6 us
    dot_general x1, matrix products, body(): jnp.einsum('ikac,kcn->ian', relaid, segment * live_mask[:, :, None], prec...  53.7 us
    reduce_scatter x1, waiting for transfers between devices, body(): lax.psum_scatter(partial_value, 'row', scatter_dimension=0, tiled=True)  34.3 us
  transfers between devices with their start and end apart: 3, of which 3 were waited for; matrix products, arithmetic and copies ran while one was open for 3% of the time, Pallas kernels for 0%

commit v1 on v0

v1 whole, which is shorter than its diff:
```python
import functools

import jax
import jax.numpy as jnp
from jax import lax
from jax.experimental import pallas as pl
from jax.experimental.pallas import tpu as pltpu
from jax.sharding import PartitionSpec as P

WIDTHS = (1024, 1024, 512)
TILE = 256
LANES = 128
MIB = 1024 * 1024


def irrep_counts(vir_irrep):
    labels = jnp.arange(8, dtype=jnp.int32)
    return jnp.sum((vir_irrep[:, None] == labels[None, :]).astype(jnp.int32), axis=0)


def block_sizes(orbital_irreps, counts):
    labels = jnp.arange(8, dtype=jnp.int32)
    return jnp.sum(
        jnp.where(orbital_irreps[:, None] == labels[None, :], counts[None, :], 0), axis=1
    )


def masks(slot_total, local_orbitals, local_columns, occ_irrep, vir_irrep):
    occupied = occ_irrep.shape[0]
    window_total = local_orbitals * lax.axis_size("row")
    counts = irrep_counts(vir_irrep)
    sizes = jnp.pad(block_sizes(occ_irrep, counts), (0, slot_total - occupied))
    local = lax.axis_index("col") * local_columns + jnp.arange(local_columns, dtype=jnp.int32)
    colmask = (local[None, :] < sizes[:, None]).astype(jnp.float32).reshape(1, slot_total * local_columns)
    window = lax.axis_index("row") * local_orbitals + jnp.arange(local_orbitals, dtype=jnp.int32)
    orbital = window * occupied // window_total
    matches = jnp.arange(occupied, dtype=jnp.int32)[None, :] == orbital[:, None]
    row_sizes = block_sizes(jnp.sum(jnp.where(matches, occ_irrep[None, :], 0), axis=1), counts)
    return colmask, row_sizes


def pack_kernel(order_ref, first_ref, second_ref, out_ref, *, width):
    slots, rows, columns = first_ref.shape[1:]
    per = LANES // width
    place = lax.broadcasted_iota(jnp.int32, (rows, LANES), 1) // width
    for group in range(2 * slots // per):
        for half in range(columns // LANES):
            at = slice(half * LANES, (half + 1) * LANES)
            tiles = []
            for k in range(per):
                slot = group * per + k
                ref = first_ref if slot < slots else second_ref
                tile = ref[0, slot % slots, :, at]
                tiles.append(pltpu.roll(tile, k * width, 1) if k else tile)
            span = 1
            while span < per:
                taken = place & span != 0
                tiles = [jnp.where(taken, tiles[(h + span) % per], tiles[h]) for h in range(per)]
                span *= 2
            for g in range(per):
                tile = tiles[-g % per]
                tile = pltpu.roll(tile, LANES - g * width, 1) if g else tile
                out_ref[half * per + g, :, group * LANES:(group + 1) * LANES] = tile


def pack(amplitudes, order, slots, width, orbital):
    wl, kt, al, ct = amplitudes.shape
    return pl.pallas_call(
        functools.partial(pack_kernel, width=width),
        grid_spec=pltpu.PrefetchScalarGridSpec(
            num_scalar_prefetch=1,
            grid=(kt // slots // 2,),
            in_specs=[
                pl.BlockSpec((1, slots, al, ct), lambda p, o: (orbital, o[2 * p], 0, 0)),
                pl.BlockSpec((1, slots, al, ct), lambda p, o: (orbital, o[2 * p + 1], 0, 0)),
            ],
            out_specs=pl.BlockSpec((ct // width, al, 2 * slots * width), lambda p, o: (0, 0, p)),
        ),
        out_shape=jax.ShapeDtypeStruct((ct // width, al, kt * width), jnp.float32),
        compiler_params=pltpu.CompilerParams(vmem_limit_bytes=56 * MIB),
        cost_estimate=pl.CostEstimate(
            flops=kt * al * ct, bytes_accessed=8 * kt * al * ct, transcendentals=0
        ),
    )(order, amplitudes, amplitudes)


def split(value):
    high = value.astype(jnp.bfloat16)
    return high, (value - high.astype(jnp.float32)).astype(jnp.bfloat16)


def prepare_kernel(size_ref, left_ref, mask_ref, high_ref, low_ref):
    block = left_ref.shape[0]
    row = pl.program_id(0) * block + lax.broadcasted_iota(jnp.int32, (block, 1), 0)
    keep = (row < size_ref[0]).astype(jnp.float32)
    high_ref[...], low_ref[...] = split(left_ref[...] * mask_ref[...] * keep)


def prepare(left, colmask, size):
    col, al, depth = left.shape
    rows, block = col * al, 64
    return pl.pallas_call(
        prepare_kernel,
        grid_spec=pltpu.PrefetchScalarGridSpec(
            num_scalar_prefetch=1,
            grid=(rows // block,),
            in_specs=[
                pl.BlockSpec((block, depth), lambda n, *_: (n, 0)),
                pl.BlockSpec((1, depth), lambda n, *_: (0, 0)),
            ],
            out_specs=[pl.BlockSpec((block, depth), lambda n, *_: (n, 0))] * 2,
        ),
        out_shape=[jax.ShapeDtypeStruct((rows, depth), jnp.bfloat16)] * 2,
        compiler_params=pltpu.CompilerParams(vmem_limit_bytes=56 * MIB),
        cost_estimate=pl.CostEstimate(flops=4 * rows * depth, bytes_accessed=8 * rows * depth, transcendentals=0),
    )(size, left.reshape(rows, depth), colmask)


def multiply_kernel(*refs, panels, lefts):
    order_ref, left_refs = refs[0], refs[1:1 + 2 * lefts]
    panel_refs, out_ref = refs[1 + 2 * lefts:-1], refs[-1]
    del order_ref
    high, low = split(jnp.concatenate([ref[...].reshape(ref.shape[-2:]) for ref in panel_refs], axis=0))
    dot = functools.partial(jnp.dot, preferred_element_type=jnp.float32)
    for i in range(lefts):
        left_high, left_low = left_refs[2 * i], left_refs[2 * i + 1]
        total = dot(left_high[...], high) + (dot(left_high[...], low) + dot(left_low[...], high))
        out_ref[:, i] = total.reshape(out_ref.shape[0], *out_ref.shape[2:])


def multiply(order, lefts, panels, virtuals):
    rows, depth = lefts[0].shape
    width = panels[0].shape[-1]
    count = len(lefts) // 2
    if len(panels) == 1:
        blocks = panels[0].shape[0]
        panels = panels * blocks
        specs = [
            pl.BlockSpec((1, depth // blocks, TILE), lambda n, o, i=i: (o[i], 0, n)) for i in range(blocks)
        ]
    else:
        specs = [pl.BlockSpec((panel.shape[0], TILE), lambda n, o: (0, n)) for panel in panels]
    shape = (rows // virtuals, count, virtuals)
    return pl.pallas_call(
        functools.partial(multiply_kernel, panels=len(panels), lefts=count),
        grid_spec=pltpu.PrefetchScalarGridSpec(
            num_scalar_prefetch=1,
            grid=(width // TILE,),
            in_specs=[pl.BlockSpec((rows, depth), lambda n, o: (0, 0))] * (2 * count) + specs,
            out_specs=pl.BlockSpec((*shape, TILE), lambda n, o: (0, 0, 0, n)),
        ),
        out_shape=jax.ShapeDtypeStruct((*shape, width), jnp.float32),
        compiler_params=pltpu.CompilerParams(vmem_limit_bytes=56 * MIB),
        cost_estimate=pl.CostEstimate(
            flops=6 * count * rows * depth * width,
            bytes_accessed=4 * (count * rows * depth + depth * width + count * rows * width),
            transcendentals=0,
        ),
    )(order, *lefts, *panels)


def body(amplitudes, integrals, occ_irrep, vir_irrep):
    rows, col = lax.axis_size("row"), lax.axis_size("col")
    wl, kt, al, ct = amplitudes.shape
    kl, cl, nt = integrals.shape
    chips = rows // 2
    here = lax.axis_index("row")
    chip, core = here // 2, here % 2
    order = jnp.stack(
        [(chip + s) % chips * 2 + c for c in (core, 1 - core) for s in (0, chips - 1, 1, 2)]
    ).astype(jnp.int32)
    colmask, row_sizes = masks(kt, wl, cl, occ_irrep, vir_irrep)
    colmask = colmask.reshape(rows, kl * cl)
    colmask = jnp.concatenate([lax.dynamic_slice_in_dim(colmask, order[i], 1) for i in range(rows)], axis=1)
    starts = [sum(WIDTHS[:i]) for i in range(len(WIDTHS))]
    own = [integrals[:, :, s:s + n] for s, n in zip(starts, WIDTHS)]

    def to_rows(value):
        return lax.all_to_all(value, "col", split_axis=0, concat_axis=0, tiled=True)

    panels = [lax.all_gather(value, "row", axis=0, tiled=True).reshape(rows, kl * cl, -1) for value in own]
    halves = []
    for w in range(wl):
        left = to_rows(pack(amplitudes, order, kl, cl, w))
        halves += prepare(left, colmask, row_sizes[w:w + 1])
    pieces = []
    for panel in panels:
        pieces.append(jnp.sum(to_rows(multiply(order, halves, [panel], al)), axis=0))
    return jnp.concatenate(pieces, axis=2)


def solution(mesh):
    return jax.shard_map(
        body,
        mesh=mesh,
        in_specs=(P("row", None, "col", None), P("row", "col", None), P(), P()),
        out_specs=P("row", "col", None),
        check_vma=False,
    )
```

time: 403 us -> 231 us (0.57)
  waiting for transfers between devices: 316 us -> 114 us
  Pallas kernels: 0 us -> 60.4 us
  matrix products: 53.7 us -> 0 us
  starting transfers between devices: 5.57 us -> 30.3 us
    all_gather x1 -> x3, waiting for transfers between devices: 220 us -> 24.7 us  [body(): lax.all_gather(value, 'row', axis=0, tiled=True).reshape(rows, kl * cl, -1)]
    pallas_call x0 -> x7, Pallas kernels: none -> 60.4 us  [the longest x3 38.3 us: multiply(): pl.pallas_call(functools.partial(multiply_kernel, panels=len(panels), lef...]
    dot_general x1 -> x0, matrix products: 53.7 us -> none  [body(): jnp.einsum('ikac,kcn->ian', relaid, segment * live_mask[:, :, None], prec...]
    reduce_scatter x1 -> x0, waiting for transfers between devices: 34.3 us -> none  [body(): lax.psum_scatter(partial_value, 'row', scatter_dimension=0, tiled=True)]
    all_to_all x1 -> x5, waiting for transfers between devices: 60.6 us -> 88.2 us  [to_rows(): return lax.all_to_all(value, 'col', split_axis=0, concat_axis=0, tiled=True)]
    all_to_all x1 -> x5, starting transfers between devices: 5.53 us -> 30.2 us  [to_rows(): return lax.all_to_all(value, 'col', split_axis=0, concat_axis=0, tiled=True)]
    slice x0 -> x3, local copies, waits for them, and re-layouts: none -> 6.18 us  [the longest x2 5.51 us: body(): own = [integrals[:, :, s:s + n] for s, n in zip(starts, WIDTHS)]]
    all_to_all x1 -> x0, local copies, waits for them, and re-layouts: 5.64 us -> none  [body(): lax.all_to_all(amplitudes, 'row', split_axis=1, concat_axis=0, tiled=True)]
  transfers between devices with their start and end apart: 3 -> 8, of which waited for: 3 -> 4; matrix products, arithmetic and copies ran while one was open for 3% -> 3% of each run, Pallas kernels for 0% -> 26%
where the time goes in v1:
time: 231 us; the launch traced here: 230 us
  waiting for transfers between devices  114 us (49%)
  Pallas kernels  60.4 us (26%)
  starting transfers between devices  30.3 us (13%)
  between operations  13.4 us (6%)
  local copies, waits for them, and re-layouts  9.33 us (4%)
  other arithmetic  3.25 us (1%)
    all_to_all x5, waiting for transfers between devices, to_rows(): return lax.all_to_all(value, 'col', split_axis=0, concat_axis=0, tiled=True)  88.2 us
    pallas_call x3, Pallas kernels, multiply(): pl.pallas_call(functools.partial(multiply_kernel, panels=len(panels), lef...  38.3 us
    all_to_all x5, starting transfers between devices, to_rows(): return lax.all_to_all(value, 'col', split_axis=0, concat_axis=0, tiled=True)  30.2 us
    all_gather x3, waiting for transfers between devices, body(): lax.all_gather(value, 'row', axis=0, tiled=True).reshape(rows, kl * cl, -1)  24.7 us
    pallas_call x2, Pallas kernels, pack(): pl.pallas_call(functools.partial(pack_kernel, width=width), grid_spec=plt...  12.7 us
    pallas_call x2, Pallas kernels, prepare(): pl.pallas_call(prepare_kernel, grid_spec=pltpu.PrefetchScalarGridSpec(num...  9.44 us
    slice x2, local copies, waits for them, and re-layouts, body(): own = [integrals[:, :, s:s + n] for s, n in zip(starts, WIDTHS)]  5.51 us
  transfers between devices with their start and end apart: 8, of which 4 were waited for; matrix products, arithmetic and copies ran while one was open for 3% of the time, Pallas kernels for 26%

profile of v1, /device:TPU:0, one launch (start us, length us, event | category | flops | bytes accessed | tf_op | source)
XLA Modules:
  0.0 230.4 jit_solution(9941114453978760721)
XLA Ops:
  6.5 2.0 slice.19
  8.6 3.5 %fusion.2 = (f32[20,16,1024]{2,1,0:T(8,128)}, f32[20,16,1024]{2,1,0:T(8,128)}) fusion(f32[20,16,2560]{2,1,0:T(8,128)} %param.5), kind=kLoop, calls=%fused_computation.23 | loop fusion | bytes 5242880 | tf_op jit(solution)/shard_map/slice | solution.py:176
  12.2 0.7 all-gather.6.cloned.1.call-update
  13.6 6.3 %shard_map.48 = f32[16,16,2560]{2,1,0:T(8,128)} custom-call(s32[8]{0:T(128)} %stack.35.order_ref.refs_0_, f32[2,160,16,256]{3,2,1,0:T(8,128)} %second_ref.3, f32[2,160,16,256]{3,2,1,0:T(8,128)} %second_ref.3), custom_call_target="tpu_custom_call" | custom-call | flops 655360 | bytes 5242880 | tf_op jit(solution)/shard_map/pallas_call | solution.py:68
  19.9 7.1 %all-to-all-start.1 = ((f32[16,16,2560]{2,1,0:T(8,128)}), f32[16,16,2560]{2,1,0:T(8,128)S(1)}, u32[]{:S(2)}, u32[]{:S(2)}) async-start(f32[16,16,2560]{2,1,0:T(8,128)} %shard_map.48), calls=%async_computation.1 | async-start | bytes 5242880 | tf_op jit(solution)/shard_map/all_to_all | solution.py:179
  27.0 6.4 %shard_map.46 = f32[16,16,2560]{2,1,0:T(8,128)} custom-call(s32[8]{0:T(128)} %stack.35.order_ref.refs_0_, f32[2,160,16,256]{3,2,1,0:T(8,128)} %second_ref.3, f32[2,160,16,256]{3,2,1,0:T(8,128)} %second_ref.3), custom_call_target="tpu_custom_call" | custom-call | flops 655360 | bytes 5242880 | tf_op jit(solution)/shard_map/pallas_call | solution.py:68
  33.4 30.7 %all-to-all-done.1 = f32[16,16,2560]{2,1,0:T(8,128)S(1)} async-done(((f32[16,16,2560]{2,1,0:T(8,128)}), f32[16,16,2560]{2,1,0:T(8,128)S(1)}, u32[]{:S(2)}, u32[]{:S(2)}) %all-to-all-start.1) | async-done | bytes 2621472 | tf_op jit(solution)/shard_map/all_to_all | solution.py:179
  64.1 1.5 copy-done
  65.6 4.5 %all-to-all-start = ((f32[16,16,2560]{2,1,0:T(8,128)}), f32[16,16,2560]{2,1,0:T(8,128)}, u32[]{:S(2)}, u32[]{:S(2)}) async-start(f32[16,16,2560]{2,1,0:T(8,128)} %shard_map.46), calls=%async_computation | async-start | bytes 5242880 | tf_op jit(solution)/shard_map/all_to_all | solution.py:179
  70.7 0.7 concatenate.6.mask_ref
  71.8 0.7 fusion.3
  72.5 4.8 %shard_map.49 = (bf16[256,2560]{1,0:T(8,128)(2,1)}, bf16[256,2560]{1,0:T(8,128)(2,1)}) custom-call(s32[1]{0:T(128)} %get-tuple-element.23.size_ref, f32[256,2560]{1,0:T(8,128)} %bitcast.37, f32[1,2560]{1,0:T(1,128)} %concatenate.6.mask_ref), custom_call_target="tpu_custom_call" | custom-call | flops 2621440 | bytes 5242880 | tf_op jit(solution)/shard_map/pallas_call | solution.py:102
  77.3 26.8 %all-to-all-done = f32[16,16,2560]{2,1,0:T(8,128)} async-done(((f32[16,16,2560]{2,1,0:T(8,128)}), f32[16,16,2560]{2,1,0:T(8,128)}, u32[]{:S(2)}, u32[]{:S(2)}) %all-to-all-start) | async-done | bytes 2621472 | tf_op jit(solution)/shard_map/all_to_all | solution.py:179
  104.0 4.7 %shard_map.47 = (bf16[256,2560]{1,0:T(8,128)(2,1)}, bf16[256,2560]{1,0:T(8,128)(2,1)}) custom-call(s32[1]{0:T(128)} %get-tuple-element.24.size_ref, f32[256,2560]{1,0:T(8,128)} %bitcast.8.left_ref, f32[1,2560]{1,0:T(1,128)} %concatenate.6.mask_ref), custom_call_target="tpu_custom_call" | custom-call | flops 2621440 | bytes 5242880 | tf_op jit(solution)/shard_map/pallas_call | solution.py:102
  108.7 9.6 %shard_map.52 = f32[16,2,16,512]{3,2,1,0:T(8,128)} custom-call(s32[8]{0:T(128)} %stack.35.order_ref.refs_0_, bf16[256,2560]{1,0:T(8,128)(2,1)} %get-tuple-element.9.refs_1_, bf16[256,2560]{1,0:T(8,128)(2,1)} %get-tuple-element.10.refs_2_, bf16[256,2560]{1,0:T(8,128)(2,1)} %get-tuple-element.11.refs_3_, bf16[256,2560]{1,0:T(8,128)(2,1)} %get-tuple-element.12.refs_4_, ...), custom_call_target="tpu_custom_call" | custom-call | flops 4026531840 | bytes 11534336 | tf_op jit(solution)/shard_map/pallas_call | solution.py:144
  118.4 4.6 %all-to-all-start.4 = ((f32[16,2,16,512]{3,2,1,0:T(8,128)}), f32[16,2,16,512]{3,2,1,0:T(8,128)S(1)}, u32[]{:S(2)}, u32[]{:S(2)}) async-start(f32[16,2,16,512]{3,2,1,0:T(8,128)} %shard_map.52), calls=%async_computation.4 | async-start | bytes 2097152 | tf_op jit(solution)/shard_map/all_to_all | solution.py:179
  123.0 14.3 %shard_map.50 = f32[16,2,16,1024]{3,2,1,0:T(8,128)} custom-call(s32[8]{0:T(128)} %stack.35.order_ref.refs_0_, bf16[256,2560]{1,0:T(8,128)(2,1)} %get-tuple-element.9.refs_1_, bf16[256,2560]{1,0:T(8,128)(2,1)} %get-tuple-element.10.refs_2_, bf16[256,2560]{1,0:T(8,128)(2,1)} %get-tuple-element.11.refs_3_, bf16[256,2560]{1,0:T(8,128)(2,1)} %get-tuple-element.12.refs_4_, ...), custom_call_target="tpu_custom_call" | custom-call | flops 8053063680 | bytes 17825792 | tf_op jit(solution)/shard_map/pallas_call | solution.py:144
  137.3 7.2 %all-to-all-start.2 = ((f32[16,2,16,1024]{3,2,1,0:T(8,128)}), f32[16,2,16,1024]{3,2,1,0:T(8,128)S(1)}, u32[]{:S(2)}, u32[]{:S(2)}) async-start(f32[16,2,16,1024]{3,2,1,0:T(8,128)} %shard_map.50), calls=%async_computation.2 | async-start | bytes 4194304 | tf_op jit(solution)/shard_map/all_to_all | solution.py:179
  144.5 24.7 %all-gather.6.cloned.1.call-done = f32[160,16,1024]{2,1,0:T(8,128)} async-done(((f32[20,16,1024]{2,1,0:T(8,128)}), f32[160,16,1024]{2,1,0:T(8,128)}) %all-gather.6.cloned.1.call-update) | async-done | bytes 10485776 | tf_op jit(solution)/shard_map/all_gather | solution.py:181
  169.2 14.3 %shard_map.51 = f32[16,2,16,1024]{3,2,1,0:T(8,128)} custom-call(s32[8]{0:T(128)} %stack.35.order_ref.refs_0_, bf16[256,2560]{1,0:T(8,128)(2,1)} %get-tuple-element.9.refs_1_, bf16[256,2560]{1,0:T(8,128)(2,1)} %get-tuple-element.10.refs_2_, bf16[256,2560]{1,0:T(8,128)(2,1)} %get-tuple-element.11.refs_3_, bf16[256,2560]{1,0:T(8,128)(2,1)} %get-tuple-element.12.refs_4_, ...), custom_call_target="tpu_custom_call" | custom-call | flops 8053063680 | bytes 17825792 | tf_op jit(solution)/shard_map/pallas_call | solution.py:144
  183.5 6.9 %all-to-all-start.3 = ((f32[16,2,16,1024]{3,2,1,0:T(8,128)}), f32[16,2,16,1024]{3,2,1,0:T(8,128)}, u32[]{:S(2)}, u32[]{:S(2)}) async-start(f32[16,2,16,1024]{3,2,1,0:T(8,128)} %shard_map.51), calls=%async_computation.3 | async-start | bytes 4194304 | tf_op jit(solution)/shard_map/all_to_all | solution.py:179
  190.6 30.8 %all-to-all-done.3 = f32[16,2,16,1024]{3,2,1,0:T(8,128)} async-done(((f32[16,2,16,1024]{3,2,1,0:T(8,128)}), f32[16,2,16,1024]{3,2,1,0:T(8,128)}, u32[]{:S(2)}, u32[]{:S(2)}) %all-to-all-start.3) | async-done | bytes 2097184 | tf_op jit(solution)/shard_map/all_to_all | solution.py:179
  221.4 1.7 reduce_sum.68
  223.1 0.7 pad_maximum_fusion
  (31 shorter events, 1.9 us)
Async XLA Ops:
  6.5 102.2 %all-gather.8.cloned.1.call-start = ((), (), s32[]{:S(2)}) async-start(), calls=%async_computation.7 | async-start | bytes 5898240 | tf_op jit(solution)/shard_map/all_gather | solution.py:181
  8.5 114.4 %all-gather.4.cloned.1.call-start = ((), (), s32[]{:S(2)}) async-start(), calls=%async_computation.5 | async-start | bytes 11796480 | tf_op jit(solution)/shard_map/all_gather | solution.py:181
  12.1 157.1 %all-gather.6.cloned.1.call-start = ((), (), s32[]{:S(2)}) async-start(), calls=%async_computation.6 | async-start | bytes 11796480 | tf_op jit(solution)/shard_map/all_gather | solution.py:181
  19.9 44.2 %all-to-all-start.1 = ((f32[16,16,2560]{2,1,0:T(8,128)}), f32[16,16,2560]{2,1,0:T(8,128)S(1)}, u32[]{:S(2)}, u32[]{:S(2)}) async-start(f32[16,16,2560]{2,1,0:T(8,128)} %shard_map.48), calls=%async_computation.1 | async-start | bytes 5242880 | tf_op jit(solution)/shard_map/all_to_all | solution.py:179
  33.4 36.7 %copy-start.1 = (s32[1500]{0:T(1024)S(1)}, s32[1500]{0:T(1024)}, u32[]{:S(2)}) copy-start(s32[1500]{0:T(1024)} %param.7) | copy-start | bytes 18004
  33.4 36.8 %copy-start.2 = (s32[150]{0:T(256)S(1)}, s32[150]{0:T(256)}, u32[]{:S(2)}) copy-start(s32[150]{0:T(256)} %param.6) | copy-start | bytes 1804
  64.1 1.5 copy-start
  65.6 38.5 %all-to-all-start = ((f32[16,16,2560]{2,1,0:T(8,128)}), f32[16,16,2560]{2,1,0:T(8,128)}, u32[]{:S(2)}, u32[]{:S(2)}) async-start(f32[16,16,2560]{2,1,0:T(8,128)} %shard_map.46), calls=%async_computation | async-start | bytes 5242880 | tf_op jit(solution)/shard_map/all_to_all | solution.py:179
  118.4 19.0 %all-to-all-start.4 = ((f32[16,2,16,512]{3,2,1,0:T(8,128)}), f32[16,2,16,512]{3,2,1,0:T(8,128)S(1)}, u32[]{:S(2)}, u32[]{:S(2)}) async-start(f32[16,2,16,512]{3,2,1,0:T(8,128)} %shard_map.52), calls=%async_computation.4 | async-start | bytes 2097152 | tf_op jit(solution)/shard_map/all_to_all | solution.py:179
  137.3 46.2 %all-to-all-start.2 = ((f32[16,2,16,1024]{3,2,1,0:T(8,128)}), f32[16,2,16,1024]{3,2,1,0:T(8,128)S(1)}, u32[]{:S(2)}, u32[]{:S(2)}) async-start(f32[16,2,16,1024]{3,2,1,0:T(8,128)} %shard_map.50), calls=%async_computation.2 | async-start | bytes 4194304 | tf_op jit(solution)/shard_map/all_to_all | solution.py:179
  183.5 37.8 %all-to-all-start.3 = ((f32[16,2,16,1024]{3,2,1,0:T(8,128)}), f32[16,2,16,1024]{3,2,1,0:T(8,128)}, u32[]{:S(2)}, u32[]{:S(2)}) async-start(f32[16,2,16,1024]{3,2,1,0:T(8,128)} %shard_map.51), calls=%async_computation.3 | async-start | bytes 4194304 | tf_op jit(solution)/shard_map/all_to_all | solution.py:179
Sparse Core Ops, SparseCore 0:
  9.0 39.1 all-gather.7
  50.0 58.5 all-gather.3
  110.3 58.8 all-gather.5

commit v2 on v1

--- a/solution.py
+++ b/solution.py
@@ -7,7 +7,7 @@
 from jax.experimental.pallas import tpu as pltpu
 from jax.sharding import PartitionSpec as P
 
-WIDTHS = (1024, 1024, 512)
+WIDTHS = (1536, 1024)
 TILE = 256
 LANES = 128
 MIB = 1024 * 1024
@@ -98,7 +98,7 @@
 
 def prepare(left, colmask, size):
     col, al, depth = left.shape
-    rows, block = col * al, 64
+    rows, block = col * al, 128
     return pl.pallas_call(
         prepare_kernel,
         grid_spec=pltpu.PrefetchScalarGridSpec(
@@ -163,30 +163,63 @@
     rows, col = lax.axis_size("row"), lax.axis_size("col")
     wl, kt, al, ct = amplitudes.shape
     kl, cl, nt = integrals.shape
-    chips = rows // 2
+    part, chips = kl // 2, rows // 2
+    cross = [(r, r ^ 1) for r in range(rows)]
+    up = [(r, (r + 2) % rows) for r in range(rows)]
+    down = [(r, (r - 2) % rows) for r in range(rows)]
     here = lax.axis_index("row")
     chip, core = here // 2, here % 2
     order = jnp.stack(
         [(chip + s) % chips * 2 + c for c in (core, 1 - core) for s in (0, chips - 1, 1, 2)]
     ).astype(jnp.int32)
+
+    def to_rows(value):
+        return lax.all_to_all(value, "col", split_axis=0, concat_axis=0, tiled=True)
+
+    def ring(value):
+        return [lax.ppermute(value, "row", up), lax.ppermute(value, "row", down)]
+
+    def ring_on(near):
+        return [lax.ppermute(near[0][:part], "row", up), lax.ppermute(near[1][part:], "row", down)]
+
+    def other_core(values):
+        return [lax.ppermute(value, "row", cross) for value in values]
+
+    def flat(*panels):
+        return [panel.reshape(-1, panel.shape[-1]) for panel in panels]
+
+    packed = [pack(amplitudes, order, kl, cl, w) for w in range(wl)]
+    late, early = integrals[:, :, :WIDTHS[1]], integrals[:, :, WIDTHS[1]:]
+    near0 = ring(early)
+    near0, packed[1] = lax.optimization_barrier((near0, packed[1]))
+    far0 = ring_on(near0)
+    over0 = other_core([early, *near0])
+    (late, far0, over0) = lax.optimization_barrier((late, far0, over0))
+    near1 = ring(late)
+    over0 += other_core(far0)
     colmask, row_sizes = masks(kt, wl, cl, occ_irrep, vir_irrep)
     colmask = colmask.reshape(rows, kl * cl)
     colmask = jnp.concatenate([lax.dynamic_slice_in_dim(colmask, order[i], 1) for i in range(rows)], axis=1)
-    starts = [sum(WIDTHS[:i]) for i in range(len(WIDTHS))]
-    own = [integrals[:, :, s:s + n] for s, n in zip(starts, WIDTHS)]
-
-    def to_rows(value):
-        return lax.all_to_all(value, "col", split_axis=0, concat_axis=0, tiled=True)
-
-    panels = [lax.all_gather(value, "row", axis=0, tiled=True).reshape(rows, kl * cl, -1) for value in own]
-    halves = []
-    for w in range(wl):
-        left = to_rows(pack(amplitudes, order, kl, cl, w))
-        halves += prepare(left, colmask, row_sizes[w:w + 1])
-    pieces = []
-    for panel in panels:
-        pieces.append(jnp.sum(to_rows(multiply(order, halves, [panel], al)), axis=0))
-    return jnp.concatenate(pieces, axis=2)
+    left0 = to_rows(packed[0])
+    packed[1], left0 = lax.optimization_barrier((packed[1], left0))
+    left1 = to_rows(packed[1])
+    halves = prepare(left0, colmask, row_sizes[0:1])
+    panels = flat(early, *near0, *far0, *over0)
+    piece0 = multiply(order, halves, panels, al)
+    moved0 = to_rows(lax.optimization_barrier((piece0, left1))[0])
+    halves = halves + prepare(left1, colmask, row_sizes[1:2])
+    piece1 = multiply(order, halves[2:], panels, al)
+    near1 = lax.optimization_barrier((near1, piece0, halves[2:]))[0]
+    far1 = ring_on(near1)
+    over1 = other_core([late, *near1])
+    far1 = lax.optimization_barrier((far1, piece1))[0]
+    over1 += other_core(far1)
+    moved1 = to_rows(lax.optimization_barrier((piece1, moved0))[0])
+    last = multiply(order, halves, flat(late, *near1, *far1, *over1), al)
+    last = lax.optimization_barrier((last, moved1))[0]
+    sums = [jnp.sum(moved, axis=0) for moved in (moved0, moved1)]
+    last = jnp.sum(to_rows(last), axis=0)
+    return jnp.concatenate([last, jnp.concatenate(sums, axis=0)], axis=2)
 
 
 def solution(mesh):

time: 231 us -> 208 us (0.900)
  waiting for transfers between devices: 114 us -> 73 us
  starting transfers between devices: 30.3 us -> 48 us
  between operations: 13.4 us -> 0.26 us
  local copies, waits for them, and re-layouts: 9.33 us -> 21.1 us
    all_to_all x5, waiting for transfers between devices: 88.2 us -> 32.8 us  [to_rows(): return lax.all_to_all(value, 'col', split_axis=0, concat_axis=0, tiled=True)]
    ppermute x0 -> x18, waiting for transfers between devices: none -> 40.2 us  [the longest x4 26.9 us: ring(): return [lax.ppermute(value, 'row', up), lax.ppermute(value, 'row', down)]]
    all_gather x3 -> x0, waiting for transfers between devices: 24.7 us -> none  [body(): lax.all_gather(value, 'row', axis=0, tiled=True).reshape(rows, kl * cl, -1)]
    ppermute x0 -> x18, starting transfers between devices: none -> 16.1 us  [the longest x4 7.36 us: ring(): return [lax.ppermute(value, 'row', up), lax.ppermute(value, 'row', down)]]
    slice x3 -> x7, local copies, waits for them, and re-layouts: 6.18 us -> 14.6 us  [the longest x2 5.56 us: body(): late, early = (integrals[:, :, :WIDTHS[1]], integrals[:, :, WIDTHS[1]:])]
    unnamed x6 -> x18, local copies, waits for them, and re-layouts: 1.49 us -> 4.77 us
    pallas_call x2, Pallas kernels: 9.44 us -> 7.09 us  [prepare(): pl.pallas_call(prepare_kernel, grid_spec=pltpu.PrefetchScalarGridSpec(num...]
  transfers between devices with their start and end apart: 8 -> 23, of which waited for: 4 -> 7; matrix products, arithmetic and copies ran while one was open for 3% -> 8% of each run, Pallas kernels for 26% -> 29%
where the time goes in v2:
time: 208 us; the launch traced here: 207 us
  waiting for transfers between devices  73 us (35%)
  Pallas kernels  59.9 us (29%)
  starting transfers between devices  48 us (23%)
  local copies, waits for them, and re-layouts  21.1 us (10%)
  other arithmetic  4.46 us (2%)
    pallas_call x3, Pallas kernels, multiply(): pl.pallas_call(functools.partial(multiply_kernel, panels=len(panels), lef...  40.1 us
    all_to_all x5, waiting for transfers between devices, to_rows(): return lax.all_to_all(value, 'col', split_axis=0, concat_axis=0, tiled=True)  32.8 us
    all_to_all x5, starting transfers between devices, to_rows(): return lax.all_to_all(value, 'col', split_axis=0, concat_axis=0, tiled=True)  31.9 us
    ppermute x4, waiting for transfers between devices, ring(): return [lax.ppermute(value, 'row', up), lax.ppermute(value, 'row', down)]  26.9 us
    pallas_call x2, Pallas kernels, pack(): pl.pallas_call(functools.partial(pack_kernel, width=width), grid_spec=plt...  12.7 us
    ppermute x2, waiting for transfers between devices, ring_on(): lax.ppermute(near[0][:part], 'row', up)  10.6 us
    ppermute x4, starting transfers between devices, ring(): return [lax.ppermute(value, 'row', up), lax.ppermute(value, 'row', down)]  7.36 us
    pallas_call x2, Pallas kernels, prepare(): pl.pallas_call(prepare_kernel, grid_spec=pltpu.PrefetchScalarGridSpec(num...  7.09 us
  transfers between devices with their start and end apart: 23, of which 7 were waited for; matrix products, arithmetic and copies ran while one was open for 8% of the time, Pallas kernels for 29%

profile of v2, /device:TPU:0, one launch (start us, length us, event | category | flops | bytes accessed | tf_op | source)
XLA Modules:
  0.0 206.7 jit_solution(15016748004486842593)
XLA Ops:
  0.0 3.0 %slice.25 = f32[20,16,1536]{2,1,0:T(8,128)} slice(f32[20,16,2560]{2,1,0:T(8,128)} %param.5), slice={[0:20], [0:16], [1024:2560]} | slice | bytes 3932160 | tf_op jit(solution)/shard_map/slice | solution.py:192
  3.0 2.0 collective-permute-start
  5.0 2.1 %collective-permute-start.1 = (f32[20,16,1536]{2,1,0:T(8,128)}, f32[20,16,1536]{2,1,0:T(8,128)}, u32[]{:S(2)}, u32[]{:S(2)}) collective-permute-start(f32[20,16,1536]{2,1,0:T(8,128)} %slice.25), channel_id=1, source_target_pairs={{0,96},{16,112},{32,0},{48,16},{64,32},{80,48},{96,64},{112,80},{1... | collective-permute-start | bytes 5898248 | tf_op jit(solution)/shard_map/ppermute | solution.py:180
  7.7 6.4 %shard_map.47 = f32[16,16,2560]{2,1,0:T(8,128)} custom-call(s32[8]{0:T(128)} %stack.35.order_ref.refs_0_, f32[2,160,16,256]{3,2,1,0:T(8,128)} %second_ref.3, f32[2,160,16,256]{3,2,1,0:T(8,128)} %second_ref.3), custom_call_target="tpu_custom_call" | custom-call | flops 655360 | bytes 5242880 | tf_op jit(solution)/shard_map/pallas_call | solution.py:68
  14.1 7.0 %all-to-all-start = ((f32[16,16,2560]{2,1,0:T(8,128)}), f32[16,16,2560]{2,1,0:T(8,128)S(1)}, u32[]{:S(2)}, u32[]{:S(2)}) async-start(f32[16,16,2560]{2,1,0:T(8,128)} %shard_map.47), calls=%async_computation | async-start | bytes 5242880 | tf_op jit(solution)/shard_map/all_to_all | solution.py:177
  21.2 6.3 %shard_map.46 = f32[16,16,2560]{2,1,0:T(8,128)} custom-call(s32[8]{0:T(128)} %stack.35.order_ref.refs_0_, f32[2,160,16,256]{3,2,1,0:T(8,128)} %second_ref.3, f32[2,160,16,256]{3,2,1,0:T(8,128)} %second_ref.3), custom_call_target="tpu_custom_call" | custom-call | flops 655360 | bytes 5242880 | tf_op jit(solution)/shard_map/pallas_call | solution.py:68
  27.6 22.7 %collective-permute-done = f32[20,16,1536]{2,1,0:T(8,128)} collective-permute-done((f32[20,16,1536]{2,1,0:T(8,128)}, f32[20,16,1536]{2,1,0:T(8,128)}, u32[]{:S(2)}, u32[]{:S(2)}) %collective-permute-start) | collective-permute-done | bytes 1966112 | tf_op jit(solution)/shard_map/ppermute | solution.py:180
  50.8 2.2 %slice.28 = f32[10,16,1536]{2,1,0:T(8,128)} slice(f32[20,16,1536]{2,1,0:T(8,128)} %collective-permute-done), slice={[0:10], [0:16], [0:1536]} | slice | bytes 1966080 | tf_op jit(solution)/shard_map/slice | solution.py:183
  53.0 2.2 %slice.29 = f32[10,16,1536]{2,1,0:T(8,128)} slice(f32[20,16,1536]{2,1,0:T(8,128)} %collective-permute-done.1), slice={[10:20], [0:16], [0:1536]} | slice | bytes 1966080 | tf_op jit(solution)/shard_map/slice | solution.py:183
  60.0 7.1 %all-to-all-start.1 = ((f32[16,16,2560]{2,1,0:T(8,128)}), f32[16,16,2560]{2,1,0:T(8,128)}, u32[]{:S(2)}, u32[]{:S(2)}) async-start(f32[16,16,2560]{2,1,0:T(8,128)} %shard_map.46), calls=%async_computation.1 | async-start | bytes 5242880 | tf_op jit(solution)/shard_map/all_to_all | solution.py:177
  67.1 2.5 %slice.27 = f32[20,16,1024]{2,1,0:T(8,128)} slice(f32[20,16,2560]{2,1,0:T(8,128)} %param.5), slice={[0:20], [0:16], [0:1024]} | slice | bytes 2621440 | tf_op jit(solution)/shard_map/slice | solution.py:192
  69.8 10.6 %collective-permute-done.2 = f32[10,16,1536]{2,1,0:T(8,128)} collective-permute-done((f32[10,16,1536]{2,1,0:T(8,128)}, f32[10,16,1536]{2,1,0:T(8,128)}, u32[]{:S(2)}, u32[]{:S(2)}) %collective-permute-start.2) | collective-permute-done | bytes 983072 | tf_op jit(solution)/shard_map/ppermute | solution.py:183
  83.2 3.5 %shard_map.48 = (bf16[256,2560]{1,0:T(8,128)(2,1)}, bf16[256,2560]{1,0:T(8,128)(2,1)}) custom-call(s32[1]{0:T(128)} %get-tuple-element.57.size_ref, f32[256,2560]{1,0:T(8,128)} %bitcast.32, f32[1,2560]{1,0:T(1,128)} %concatenate.9.mask_ref), custom_call_target="tpu_custom_call" | custom-call | flops 2621440 | bytes 5242880 | tf_op jit(solution)/shard_map/pallas_call | solution.py:102
  91.2 13.0 %shard_map.50 = f32[16,1,16,1536]{3,2,1,0:T(8,128)} custom-call(s32[8]{0:T(128)} %stack.35.order_ref.refs_0_, bf16[256,2560]{1,0:T(8,128)(2,1)} %get-tuple-element.29.refs_1_, bf16[256,2560]{1,0:T(8,128)(2,1)} %get-tuple-element.30.refs_2_, f32[320,1536]{1,0:T(8,128)} %bitcast.11.refs_3_, f32[320,1536]{1,0:T(8,128)} %bitcast.12.refs_4_, ...), custom_call_target="tpu_custom_call" | custom-call | flops 6039797760 | bytes 19922944 | tf_op jit(solution)/shard_map/pallas_call | solution.py:144
  104.2 7.0 %all-to-all-start.2 = ((f32[16,1,16,1536]{3,2,1,0:T(8,128)}), f32[16,1,16,1536]{3,2,1,0:T(8,128)S(1)}, u32[]{:S(2)}, u32[]{:S(2)}) async-start(f32[16,1,16,1536]{3,2,1,0:T(8,128)} %shard_map.50), calls=%async_computation.2 | async-start | bytes 3145728 | tf_op jit(solution)/shard_map/all_to_all | solution.py:177
  111.3 3.6 %shard_map.49 = (bf16[256,2560]{1,0:T(8,128)(2,1)}, bf16[256,2560]{1,0:T(8,128)(2,1)}) custom-call(s32[1]{0:T(128)} %get-tuple-element.58.size_ref, f32[256,2560]{1,0:T(8,128)} %bitcast.9.left_ref, f32[1,2560]{1,0:T(1,128)} %concatenate.9.mask_ref), custom_call_target="tpu_custom_call" | custom-call | flops 2621440 | bytes 5242880 | tf_op jit(solution)/shard_map/pallas_call | solution.py:102
  114.8 4.2 %collective-permute-done.7 = f32[20,16,1024]{2,1,0:T(8,128)} collective-permute-done((f32[20,16,1024]{2,1,0:T(8,128)}, f32[20,16,1024]{2,1,0:T(8,128)}, u32[]{:S(2)}, u32[]{:S(2)}) %collective-permute-start.7) | collective-permute-done | bytes 1310752 | tf_op jit(solution)/shard_map/ppermute | solution.py:180
  122.3 2.0 slice.31
  126.8 12.9 %shard_map.51 = f32[16,1,16,1536]{3,2,1,0:T(8,128)} custom-call(s32[8]{0:T(128)} %stack.35.order_ref.refs_0_, bf16[256,2560]{1,0:T(8,128)(2,1)} %get-tuple-element.32.refs_1_.refs_3_, bf16[256,2560]{1,0:T(8,128)(2,1)} %get-tuple-element.33.refs_2_.refs_4_, f32[320,1536]{1,0:T(8,128)} %bitcast.11.refs_3_, f32[320,1536]{1,0:T(8,128)} %bitcast.12.refs_4_, ...), custom_call_target="tpu_custom_call" | custom-call | flops 6039797760 | bytes 19922944 | tf_op jit(solution)/shard_map/pallas_call | solution.py:144
  139.8 7.0 %all-to-all-start.3 = ((f32[16,1,16,1536]{3,2,1,0:T(8,128)}), f32[16,1,16,1536]{3,2,1,0:T(8,128)S(1)}, u32[]{:S(2)}, u32[]{:S(2)}) async-start(f32[16,1,16,1536]{3,2,1,0:T(8,128)} %shard_map.51), calls=%async_computation.3 | async-start | bytes 3145728 | tf_op jit(solution)/shard_map/all_to_all | solution.py:177
  151.0 14.2 %shard_map.52 = f32[16,2,16,1024]{3,2,1,0:T(8,128)} custom-call(s32[8]{0:T(128)} %stack.35.order_ref.refs_0_, bf16[256,2560]{1,0:T(8,128)(2,1)} %get-tuple-element.29.refs_1_, bf16[256,2560]{1,0:T(8,128)(2,1)} %get-tuple-element.30.refs_2_, bf16[256,2560]{1,0:T(8,128)(2,1)} %get-tuple-element.32.refs_1_.refs_3_, ...), custom_call_target="tpu_custom_call" | custom-call | flops 8053063680 | bytes 17825792 | tf_op jit(solution)/shard_map/pallas_call | solution.py:144
  165.2 6.9 %all-to-all-done.3 = f32[16,1,16,1536]{3,2,1,0:T(8,128)S(1)} async-done(((f32[16,1,16,1536]{3,2,1,0:T(8,128)}), f32[16,1,16,1536]{3,2,1,0:T(8,128)S(1)}, u32[]{:S(2)}, u32[]{:S(2)}) %all-to-all-start.3) | async-done | bytes 1572896 | tf_op jit(solution)/shard_map/all_to_all | solution.py:177
  173.3 3.7 %all-to-all-start.4 = ((f32[16,2,16,1024]{3,2,1,0:T(8,128)}), f32[16,2,16,1024]{3,2,1,0:T(8,128)S(1)}, u32[]{:S(2)}, u32[]{:S(2)}) async-start(f32[16,2,16,1024]{3,2,1,0:T(8,128)} %shard_map.52), calls=%async_computation.4 | async-start | bytes 4194304 | tf_op jit(solution)/shard_map/all_to_all | solution.py:177
  180.0 25.9 %all-to-all-done.4 = f32[16,2,16,1024]{3,2,1,0:T(8,128)S(1)} async-done(((f32[16,2,16,1024]{3,2,1,0:T(8,128)}), f32[16,2,16,1024]{3,2,1,0:T(8,128)S(1)}, u32[]{:S(2)}, u32[]{:S(2)}) %all-to-all-start.4) | async-done | bytes 2097184 | tf_op jit(solution)/shard_map/all_to_all | solution.py:177
  (74 shorter events, 28.2 us)
Async XLA Ops:
  3.0 47.3 %collective-permute-start = (f32[20,16,1536]{2,1,0:T(8,128)}, f32[20,16,1536]{2,1,0:T(8,128)}, u32[]{:S(2)}, u32[]{:S(2)}) collective-permute-start(f32[20,16,1536]{2,1,0:T(8,128)} %slice.25), channel_id=1, source_target_pairs={{0,32},{16,48},{32,64},{48,80},{64,96},{80,112},{96,0},{112,16},{1... | collective-permute-start | bytes 5898248 | tf_op jit(solution)/shard_map/ppermute | solution.py:180
  5.0 45.3 %collective-permute-start.1 = (f32[20,16,1536]{2,1,0:T(8,128)}, f32[20,16,1536]{2,1,0:T(8,128)}, u32[]{:S(2)}, u32[]{:S(2)}) collective-permute-start(f32[20,16,1536]{2,1,0:T(8,128)} %slice.25), channel_id=1, source_target_pairs={{0,96},{16,112},{32,0},{48,16},{64,32},{80,48},{96,64},{112,80},{1... | collective-permute-start | bytes 5898248 | tf_op jit(solution)/shard_map/ppermute | solution.py:180
  14.1 44.4 %all-to-all-start = ((f32[16,16,2560]{2,1,0:T(8,128)}), f32[16,16,2560]{2,1,0:T(8,128)S(1)}, u32[]{:S(2)}, u32[]{:S(2)}) async-start(f32[16,16,2560]{2,1,0:T(8,128)} %shard_map.47), calls=%async_computation | async-start | bytes 5242880 | tf_op jit(solution)/shard_map/all_to_all | solution.py:177
  21.1 48.7 %collective-permute-start.4 = (f32[20,16,1536]{2,1,0:T(8,128)}, f32[20,16,1536]{2,1,0:T(8,128)}, u32[]{:S(2)}, u32[]{:S(2)}) collective-permute-start(f32[20,16,1536]{2,1,0:T(8,128)} %slice.25), channel_id=1, source_target_pairs={{0,16},{16,0},{32,48},{48,32},{64,80},{80,64},{96,112},{112,96},{1... | collective-permute-start | bytes 5898248 | tf_op jit(solution)/shard_map/ppermute | solution.py:186
  50.3 30.2 %collective-permute-start.5 = (f32[20,16,1536]{2,1,0:T(8,128)}, f32[20,16,1536]{2,1,0:T(8,128)}, u32[]{:S(2)}, u32[]{:S(2)}) collective-permute-start(f32[20,16,1536]{2,1,0:T(8,128)} %collective-permute-done), channel_id=1, source_target_pairs={{0,16},{16,0},{32,48},{48,32},{64,80},{80,64},{96,112},{112,96},{1... | collective-permute-start | bytes 5898248 | tf_op jit(solution)/shard_map/ppermute | solution.py:186
  50.3 30.2 %collective-permute-start.6 = (f32[20,16,1536]{2,1,0:T(8,128)}, f32[20,16,1536]{2,1,0:T(8,128)}, u32[]{:S(2)}, u32[]{:S(2)}) collective-permute-start(f32[20,16,1536]{2,1,0:T(8,128)} %collective-permute-done.1), channel_id=1, source_target_pairs={{0,16},{16,0},{32,48},{48,32},{64,80},{80,64},{96,112},{112,96},{1... | collective-permute-start | bytes 5898248 | tf_op jit(solution)/shard_map/ppermute | solution.py:186
  55.2 25.2 %collective-permute-start.2 = (f32[10,16,1536]{2,1,0:T(8,128)}, f32[10,16,1536]{2,1,0:T(8,128)}, u32[]{:S(2)}, u32[]{:S(2)}) collective-permute-start(f32[10,16,1536]{2,1,0:T(8,128)} %slice.28), channel_id=1, source_target_pairs={{0,32},{16,48},{32,64},{48,80},{64,96},{80,112},{96,0},{112,16},{1... | collective-permute-start | bytes 2949128 | tf_op jit(solution)/shard_map/ppermute | solution.py:183
  56.5 23.9 %collective-permute-start.3 = (f32[10,16,1536]{2,1,0:T(8,128)}, f32[10,16,1536]{2,1,0:T(8,128)}, u32[]{:S(2)}, u32[]{:S(2)}) collective-permute-start(f32[10,16,1536]{2,1,0:T(8,128)} %slice.29), channel_id=1, source_target_pairs={{0,96},{16,112},{32,0},{48,16},{64,32},{80,48},{96,64},{112,80},{1... | collective-permute-start | bytes 2949128 | tf_op jit(solution)/shard_map/ppermute | solution.py:183
  60.0 44.2 %all-to-all-start.1 = ((f32[16,16,2560]{2,1,0:T(8,128)}), f32[16,16,2560]{2,1,0:T(8,128)}, u32[]{:S(2)}, u32[]{:S(2)}) async-start(f32[16,16,2560]{2,1,0:T(8,128)} %shard_map.46), calls=%async_computation.1 | async-start | bytes 5242880 | tf_op jit(solution)/shard_map/all_to_all | solution.py:177
  80.4 9.5 %collective-permute-start.9 = (f32[10,16,1536]{2,1,0:T(8,128)}, f32[10,16,1536]{2,1,0:T(8,128)S(1)}, u32[]{:S(2)}, u32[]{:S(2)}) collective-permute-start(f32[10,16,1536]{2,1,0:T(8,128)} %collective-permute-done.2), channel_id=1, source_target_pairs={{0,16},{16,0},{32,48},{48,32},{64,80},{80,64},{96,112},{112,96},{1... | collective-permute-start | bytes 2949128 | tf_op jit(solution)/shard_map/ppermute | solution.py:186
  80.5 9.4 %collective-permute-start.10 = (f32[10,16,1536]{2,1,0:T(8,128)}, f32[10,16,1536]{2,1,0:T(8,128)S(1)}, u32[]{:S(2)}, u32[]{:S(2)}) collective-permute-start(f32[10,16,1536]{2,1,0:T(8,128)} %collective-permute-done.3), channel_id=1, source_target_pairs={{0,16},{16,0},{32,48},{48,32},{64,80},{80,64},{96,112},{112,96},{1... | collective-permute-start | bytes 2949128 | tf_op jit(solution)/shard_map/ppermute | solution.py:186
  86.7 32.3 %collective-permute-start.7 = (f32[20,16,1024]{2,1,0:T(8,128)}, f32[20,16,1024]{2,1,0:T(8,128)}, u32[]{:S(2)}, u32[]{:S(2)}) collective-permute-start(f32[20,16,1024]{2,1,0:T(8,128)} %slice.27), channel_id=1, source_target_pairs={{0,32},{16,48},{32,64},{48,80},{64,96},{80,112},{96,0},{112,16},{1... | collective-permute-start | bytes 3932168 | tf_op jit(solution)/shard_map/ppermute | solution.py:180
  88.0 31.0 %collective-permute-start.8 = (f32[20,16,1024]{2,1,0:T(8,128)}, f32[20,16,1024]{2,1,0:T(8,128)}, u32[]{:S(2)}, u32[]{:S(2)}) collective-permute-start(f32[20,16,1024]{2,1,0:T(8,128)} %slice.27), channel_id=1, source_target_pairs={{0,96},{16,112},{32,0},{48,16},{64,32},{80,48},{96,64},{112,80},{1... | collective-permute-start | bytes 3932168 | tf_op jit(solution)/shard_map/ppermute | solution.py:180
  104.2 35.5 %all-to-all-start.2 = ((f32[16,1,16,1536]{3,2,1,0:T(8,128)}), f32[16,1,16,1536]{3,2,1,0:T(8,128)S(1)}, u32[]{:S(2)}, u32[]{:S(2)}) async-start(f32[16,1,16,1536]{3,2,1,0:T(8,128)} %shard_map.50), calls=%async_computation.2 | async-start | bytes 3145728 | tf_op jit(solution)/shard_map/all_to_all | solution.py:177
  121.0 25.8 %collective-permute-start.11 = (f32[10,16,1024]{2,1,0:T(8,128)}, f32[10,16,1024]{2,1,0:T(8,128)}, u32[]{:S(2)}, u32[]{:S(2)}) collective-permute-start(f32[10,16,1024]{2,1,0:T(8,128)} %slice.30), channel_id=1, source_target_pairs={{0,32},{16,48},{32,64},{48,80},{64,96},{80,112},{96,0},{112,16},{1... | collective-permute-start | bytes 1966088 | tf_op jit(solution)/shard_map/ppermute | solution.py:183
  124.3 22.5 %collective-permute-start.12 = (f32[10,16,1024]{2,1,0:T(8,128)}, f32[10,16,1024]{2,1,0:T(8,128)}, u32[]{:S(2)}, u32[]{:S(2)}) collective-permute-start(f32[10,16,1024]{2,1,0:T(8,128)} %slice.31), channel_id=1, source_target_pairs={{0,96},{16,112},{32,0},{48,16},{64,32},{80,48},{96,64},{112,80},{1... | collective-permute-start | bytes 1966088 | tf_op jit(solution)/shard_map/ppermute | solution.py:183
  126.3 21.1 %collective-permute-start.13 = (f32[20,16,1024]{2,1,0:T(8,128)}, f32[20,16,1024]{2,1,0:T(8,128)}, u32[]{:S(2)}, u32[]{:S(2)}) collective-permute-start(f32[20,16,1024]{2,1,0:T(8,128)} %slice.27), channel_id=1, source_target_pairs={{0,16},{16,0},{32,48},{48,32},{64,80},{80,64},{96,112},{112,96},{1... | collective-permute-start | bytes 3932168 | tf_op jit(solution)/shard_map/ppermute | solution.py:186
  126.3 21.1 %collective-permute-start.14 = (f32[20,16,1024]{2,1,0:T(8,128)}, f32[20,16,1024]{2,1,0:T(8,128)}, u32[]{:S(2)}, u32[]{:S(2)}) collective-permute-start(f32[20,16,1024]{2,1,0:T(8,128)} %collective-permute-done.7), channel_id=1, source_target_pairs={{0,16},{16,0},{32,48},{48,32},{64,80},{80,64},{96,112},{112,96},{1... | collective-permute-start | bytes 3932168 | tf_op jit(solution)/shard_map/ppermute | solution.py:186
  126.8 20.6 %collective-permute-start.15 = (f32[20,16,1024]{2,1,0:T(8,128)}, f32[20,16,1024]{2,1,0:T(8,128)}, u32[]{:S(2)}, u32[]{:S(2)}) collective-permute-start(f32[20,16,1024]{2,1,0:T(8,128)} %collective-permute-done.8), channel_id=1, source_target_pairs={{0,16},{16,0},{32,48},{48,32},{64,80},{80,64},{96,112},{112,96},{1... | collective-permute-start | bytes 3932168 | tf_op jit(solution)/shard_map/ppermute | solution.py:186
  139.7 25.4 %copy-start.1 = (f32[16,1,16,1536]{3,2,1,0:T(8,128)}, f32[16,1,16,1536]{3,2,1,0:T(8,128)S(1)}, u32[]{:S(2)}) copy-start(f32[16,1,16,1536]{3,2,1,0:T(8,128)S(1)} %all-to-all-done.2) | copy-start | bytes 4718596
  139.8 32.4 %all-to-all-start.3 = ((f32[16,1,16,1536]{3,2,1,0:T(8,128)}), f32[16,1,16,1536]{3,2,1,0:T(8,128)S(1)}, u32[]{:S(2)}, u32[]{:S(2)}) async-start(f32[16,1,16,1536]{3,2,1,0:T(8,128)} %shard_map.51), calls=%async_computation.3 | async-start | bytes 3145728 | tf_op jit(solution)/shard_map/all_to_all | solution.py:177
  146.8 2.4 %collective-permute-start.16 = (f32[10,16,1024]{2,1,0:T(8,128)}, f32[10,16,1024]{2,1,0:T(8,128)S(1)}, u32[]{:S(2)}, u32[]{:S(2)}) collective-permute-start(f32[10,16,1024]{2,1,0:T(8,128)} %collective-permute-done.11), channel_id=1, source_target_pairs={{0,16},{16,0},{32,48},{48,32},{64,80},{80,64},{96,112},{112,96},{1... | collective-permute-start | bytes 1966088 | tf_op jit(solution)/shard_map/ppermute | solution.py:186
  147.1 3.0 %collective-permute-start.17 = (f32[10,16,1024]{2,1,0:T(8,128)}, f32[10,16,1024]{2,1,0:T(8,128)S(1)}, u32[]{:S(2)}, u32[]{:S(2)}) collective-permute-start(f32[10,16,1024]{2,1,0:T(8,128)} %collective-permute-done.12), channel_id=1, source_target_pairs={{0,16},{16,0},{32,48},{48,32},{64,80},{80,64},{96,112},{112,96},{1... | collective-permute-start | bytes 1966088 | tf_op jit(solution)/shard_map/ppermute | solution.py:186
  173.3 32.6 %all-to-all-start.4 = ((f32[16,2,16,1024]{3,2,1,0:T(8,128)}), f32[16,2,16,1024]{3,2,1,0:T(8,128)S(1)}, u32[]{:S(2)}, u32[]{:S(2)}) async-start(f32[16,2,16,1024]{3,2,1,0:T(8,128)} %shard_map.52), calls=%async_computation.4 | async-start | bytes 4194304 | tf_op jit(solution)/shard_map/all_to_all | solution.py:177
  (8 other events, 23.2 us)

commit v3 on v2

--- a/solution.py
+++ b/solution.py
@@ -194,9 +194,6 @@
     near0, packed[1] = lax.optimization_barrier((near0, packed[1]))
     far0 = ring_on(near0)
     over0 = other_core([early, *near0])
-    (late, far0, over0) = lax.optimization_barrier((late, far0, over0))
-    near1 = ring(late)
-    over0 += other_core(far0)
     colmask, row_sizes = masks(kt, wl, cl, occ_irrep, vir_irrep)
     colmask = colmask.reshape(rows, kl * cl)
     colmask = jnp.concatenate([lax.dynamic_slice_in_dim(colmask, order[i], 1) for i in range(rows)], axis=1)
@@ -204,18 +201,22 @@
     packed[1], left0 = lax.optimization_barrier((packed[1], left0))
     left1 = to_rows(packed[1])
     halves = prepare(left0, colmask, row_sizes[0:1])
+    (far0, over0) = lax.optimization_barrier((far0, over0, halves))[:2]
+    (late, far0, over0) = lax.optimization_barrier((late, far0, over0))
+    near1 = ring(late)
+    over0 += other_core(far0)
     panels = flat(early, *near0, *far0, *over0)
     piece0 = multiply(order, halves, panels, al)
     moved0 = to_rows(lax.optimization_barrier((piece0, left1))[0])
     halves = halves + prepare(left1, colmask, row_sizes[1:2])
     piece1 = multiply(order, halves[2:], panels, al)
-    near1 = lax.optimization_barrier((near1, piece0, halves[2:]))[0]
+    near1 = lax.optimization_barrier((near1, piece1))[0]
     far1 = ring_on(near1)
     over1 = other_core([late, *near1])
     far1 = lax.optimization_barrier((far1, piece1))[0]
     over1 += other_core(far1)
+    last = multiply(order, halves, flat(late, *near1, *far1, *over1), al)
     moved1 = to_rows(lax.optimization_barrier((piece1, moved0))[0])
-    last = multiply(order, halves, flat(late, *near1, *far1, *over1), al)
     last = lax.optimization_barrier((last, moved1))[0]
     sums = [jnp.sum(moved, axis=0) for moved in (moved0, moved1)]
     last = jnp.sum(to_rows(last), axis=0)

time: 208 us -> 202 us (0.971)
  waiting for transfers between devices: 73 us -> 70.6 us
    ppermute x4, waiting for transfers between devices: 26.9 us -> 22.7 us  [ring(): return [lax.ppermute(value, 'row', up), lax.ppermute(value, 'row', down)]]
    all_to_all x5, waiting for transfers between devices: 32.8 us -> 35.1 us  [to_rows(): return lax.all_to_all(value, 'col', split_axis=0, concat_axis=0, tiled=True)]
    ppermute x2, waiting for transfers between devices: 10.6 us -> 8.53 us  [ring_on(): lax.ppermute(near[0][:part], 'row', up)]
    unnamed x18 -> x20, local copies, waits for them, and re-layouts: 4.77 us -> 4.59 us
  transfers between devices with their start and end apart: 23 -> 23, of which waited for: 7 -> 10; matrix products, arithmetic and copies ran while one was open for 8% -> 8% of each run, Pallas kernels for 29% -> 30%
where the time goes in v3:
time: 202 us; the launch traced here: 201 us
  waiting for transfers between devices  70.6 us (35%)
  Pallas kernels  60.1 us (30%)
  starting transfers between devices  46.4 us (23%)
  local copies, waits for them, and re-layouts  19.2 us (10%)
  other arithmetic  4.46 us (2%)
    pallas_call x3, Pallas kernels, multiply(): pl.pallas_call(functools.partial(multiply_kernel, panels=len(panels), lef...  40.1 us
    all_to_all x5, waiting for transfers between devices, to_rows(): return lax.all_to_all(value, 'col', split_axis=0, concat_axis=0, tiled=True)  35.1 us
    all_to_all x5, starting transfers between devices, to_rows(): return lax.all_to_all(value, 'col', split_axis=0, concat_axis=0, tiled=True)  30.2 us
    ppermute x4, waiting for transfers between devices, ring(): return [lax.ppermute(value, 'row', up), lax.ppermute(value, 'row', down)]  22.7 us
    pallas_call x2, Pallas kernels, pack(): pl.pallas_call(functools.partial(pack_kernel, width=width), grid_spec=plt...  12.7 us
    ppermute x2, waiting for transfers between devices, ring_on(): lax.ppermute(near[0][:part], 'row', up)  8.53 us
    ppermute x4, starting transfers between devices, ring(): return [lax.ppermute(value, 'row', up), lax.ppermute(value, 'row', down)]  7.36 us
    pallas_call x2, Pallas kernels, prepare(): pl.pallas_call(prepare_kernel, grid_spec=pltpu.PrefetchScalarGridSpec(num...  7.27 us
  transfers between devices with their start and end apart: 23, of which 10 were waited for; matrix products, arithmetic and copies ran while one was open for 8% of the time, Pallas kernels for 30%

profile of v3, /device:TPU:0, one launch (start us, length us, event | category | flops | bytes accessed | tf_op | source)
XLA Modules:
  0.0 200.9 jit_solution(17539366097907824328)
XLA Ops:
  0.0 3.0 %slice.25 = f32[20,16,1536]{2,1,0:T(8,128)} slice(f32[20,16,2560]{2,1,0:T(8,128)} %param.5), slice={[0:20], [0:16], [1024:2560]} | slice | bytes 3932160 | tf_op jit(solution)/shard_map/slice | solution.py:192
  7.8 6.4 %shard_map.47 = f32[16,16,2560]{2,1,0:T(8,128)} custom-call(s32[8]{0:T(128)} %stack.35.order_ref.refs_0_, f32[2,160,16,256]{3,2,1,0:T(8,128)} %second_ref.3, f32[2,160,16,256]{3,2,1,0:T(8,128)} %second_ref.3), custom_call_target="tpu_custom_call" | custom-call | flops 655360 | bytes 5242880 | tf_op jit(solution)/shard_map/pallas_call | solution.py:68
  14.1 7.0 %all-to-all-start = ((f32[16,16,2560]{2,1,0:T(8,128)}), f32[16,16,2560]{2,1,0:T(8,128)S(1)}, u32[]{:S(2)}, u32[]{:S(2)}) async-start(f32[16,16,2560]{2,1,0:T(8,128)} %shard_map.47), calls=%async_computation | async-start | bytes 5242880 | tf_op jit(solution)/shard_map/all_to_all | solution.py:177
  21.3 6.3 %shard_map.46 = f32[16,16,2560]{2,1,0:T(8,128)} custom-call(s32[8]{0:T(128)} %stack.35.order_ref.refs_0_, f32[2,160,16,256]{3,2,1,0:T(8,128)} %second_ref.3, f32[2,160,16,256]{3,2,1,0:T(8,128)} %second_ref.3), custom_call_target="tpu_custom_call" | custom-call | flops 655360 | bytes 5242880 | tf_op jit(solution)/shard_map/pallas_call | solution.py:68
  27.6 22.7 %collective-permute-done = f32[20,16,1536]{2,1,0:T(8,128)} collective-permute-done((f32[20,16,1536]{2,1,0:T(8,128)}, f32[20,16,1536]{2,1,0:T(8,128)}, u32[]{:S(2)}, u32[]{:S(2)}) %collective-permute-start) | collective-permute-done | bytes 1966112 | tf_op jit(solution)/shard_map/ppermute | solution.py:180
  50.9 2.2 %slice.28 = f32[10,16,1536]{2,1,0:T(8,128)} slice(f32[20,16,1536]{2,1,0:T(8,128)} %collective-permute-done), slice={[0:10], [0:16], [0:1536]} | slice | bytes 1966080 | tf_op jit(solution)/shard_map/slice | solution.py:183
  53.1 2.2 %slice.29 = f32[10,16,1536]{2,1,0:T(8,128)} slice(f32[20,16,1536]{2,1,0:T(8,128)} %collective-permute-done.1), slice={[10:20], [0:16], [0:1536]} | slice | bytes 1966080 | tf_op jit(solution)/shard_map/slice | solution.py:183
  60.2 7.0 %all-to-all-start.1 = ((f32[16,16,2560]{2,1,0:T(8,128)}), f32[16,16,2560]{2,1,0:T(8,128)S(1)}, u32[]{:S(2)}, u32[]{:S(2)}) async-start(f32[16,16,2560]{2,1,0:T(8,128)} %shard_map.46), calls=%async_computation.1 | async-start | bytes 5242880 | tf_op jit(solution)/shard_map/all_to_all | solution.py:177
  67.4 2.6 %slice.27 = f32[20,16,1024]{2,1,0:T(8,128)} slice(f32[20,16,2560]{2,1,0:T(8,128)} %param.5), slice={[0:20], [0:16], [0:1024]} | slice | bytes 2621440 | tf_op jit(solution)/shard_map/slice | solution.py:192
  72.1 3.6 %shard_map.48 = (bf16[256,2560]{1,0:T(8,128)(2,1)}, bf16[256,2560]{1,0:T(8,128)(2,1)}) custom-call(s32[1]{0:T(128)} %get-tuple-element.67.size_ref, f32[256,2560]{1,0:T(8,128)} %bitcast.33, f32[1,2560]{1,0:T(1,128)} %concatenate.9.mask_ref), custom_call_target="tpu_custom_call" | custom-call | flops 2621440 | bytes 5242880 | tf_op jit(solution)/shard_map/pallas_call | solution.py:102
  75.7 4.8 %collective-permute-done.2 = f32[10,16,1536]{2,1,0:T(8,128)} collective-permute-done((f32[10,16,1536]{2,1,0:T(8,128)}, f32[10,16,1536]{2,1,0:T(8,128)}, u32[]{:S(2)}, u32[]{:S(2)}) %collective-permute-start.2) | collective-permute-done | bytes 983072 | tf_op jit(solution)/shard_map/ppermute | solution.py:183
  85.8 13.0 %shard_map.52 = f32[16,1,16,1536]{3,2,1,0:T(8,128)} custom-call(s32[8]{0:T(128)} %stack.35.order_ref.refs_0_, bf16[256,2560]{1,0:T(8,128)(2,1)} %get-tuple-element.34.refs_1_, bf16[256,2560]{1,0:T(8,128)(2,1)} %get-tuple-element.35.refs_2_, f32[320,1536]{1,0:T(8,128)} %bitcast.11.refs_3_, f32[320,1536]{1,0:T(8,128)} %bitcast.12.refs_4_, ...), custom_call_target="tpu_custom_call" | custom-call | flops 6039797760 | bytes 19922944 | tf_op jit(solution)/shard_map/pallas_call | solution.py:144
  98.8 4.7 %all-to-all-done.1 = f32[16,16,2560]{2,1,0:T(8,128)S(1)} async-done(((f32[16,16,2560]{2,1,0:T(8,128)}), f32[16,16,2560]{2,1,0:T(8,128)S(1)}, u32[]{:S(2)}, u32[]{:S(2)}) %all-to-all-start.1) | async-done | bytes 2621472 | tf_op jit(solution)/shard_map/all_to_all | solution.py:177
  103.5 4.4 %all-to-all-start.2 = ((f32[16,1,16,1536]{3,2,1,0:T(8,128)}), f32[16,1,16,1536]{3,2,1,0:T(8,128)}, u32[]{:S(2)}, u32[]{:S(2)}) async-start(f32[16,1,16,1536]{3,2,1,0:T(8,128)} %shard_map.52), calls=%async_computation.2 | async-start | bytes 3145728 | tf_op jit(solution)/shard_map/all_to_all | solution.py:177
  107.9 3.6 %shard_map.49 = (bf16[256,2560]{1,0:T(8,128)(2,1)}, bf16[256,2560]{1,0:T(8,128)(2,1)}) custom-call(s32[1]{0:T(128)} %get-tuple-element.68.size_ref, f32[256,2560]{1,0:T(8,128)} %bitcast.32, f32[1,2560]{1,0:T(1,128)} %concatenate.9.mask_ref), custom_call_target="tpu_custom_call" | custom-call | flops 2621440 | bytes 5242880 | tf_op jit(solution)/shard_map/pallas_call | solution.py:102
  111.5 13.0 %shard_map.50 = f32[16,1,16,1536]{3,2,1,0:T(8,128)} custom-call(s32[8]{0:T(128)} %stack.35.order_ref.refs_0_, bf16[256,2560]{1,0:T(8,128)(2,1)} %get-tuple-element.37.refs_1_.refs_3_, bf16[256,2560]{1,0:T(8,128)(2,1)} %get-tuple-element.38.refs_2_.refs_4_, f32[320,1536]{1,0:T(8,128)} %bitcast.11.refs_3_, f32[320,1536]{1,0:T(8,128)} %bitcast.12.refs_4_, ...), custom_call_target="tpu_custom_call" | custom-call | flops 6039797760 | bytes 19922944 | tf_op jit(solution)/shard_map/pallas_call | solution.py:144
  126.9 3.3 %collective-permute-start.12 = (f32[10,16,1024]{2,1,0:T(8,128)S(1)}, f32[10,16,1024]{2,1,0:T(8,128)}, u32[]{:S(2)}, u32[]{:S(2)}) collective-permute-start(f32[10,16,1024]{2,1,0:T(8,128)S(1)} %slice.31), channel_id=1, source_target_pairs={{0,96},{16,112},{32,0},{48,16},{64,32},{80,48},{96,64},{112,80},{1... | collective-permute-start | bytes 1966088 | tf_op jit(solution)/shard_map/ppermute | solution.py:183
  130.7 7.1 %all-to-all-start.3 = ((f32[16,1,16,1536]{3,2,1,0:T(8,128)}), f32[16,1,16,1536]{3,2,1,0:T(8,128)S(1)}, u32[]{:S(2)}, u32[]{:S(2)}) async-start(f32[16,1,16,1536]{3,2,1,0:T(8,128)} %shard_map.50), calls=%async_computation.3 | async-start | bytes 3145728 | tf_op jit(solution)/shard_map/all_to_all | solution.py:177
  137.8 3.7 %collective-permute-done.11 = f32[10,16,1024]{2,1,0:T(8,128)S(1)} collective-permute-done((f32[10,16,1024]{2,1,0:T(8,128)S(1)}, f32[10,16,1024]{2,1,0:T(8,128)S(1)}, u32[]{:S(2)}, u32[]{:S(2)}) %collective-permute-start.11) | collective-permute-done | bytes 655392 | tf_op jit(solution)/shard_map/ppermute | solution.py:183
  143.1 2.5 %collective-permute-done.16 = f32[10,16,1024]{2,1,0:T(8,128)S(1)} collective-permute-done((f32[10,16,1024]{2,1,0:T(8,128)S(1)}, f32[10,16,1024]{2,1,0:T(8,128)S(1)}, u32[]{:S(2)}, u32[]{:S(2)}) %collective-permute-start.16) | collective-permute-done | bytes 655392 | tf_op jit(solution)/shard_map/ppermute | solution.py:186
  146.7 14.2 %shard_map.51 = f32[16,2,16,1024]{3,2,1,0:T(8,128)} custom-call(s32[8]{0:T(128)} %stack.35.order_ref.refs_0_, bf16[256,2560]{1,0:T(8,128)(2,1)} %get-tuple-element.34.refs_1_, bf16[256,2560]{1,0:T(8,128)(2,1)} %get-tuple-element.35.refs_2_, bf16[256,2560]{1,0:T(8,128)(2,1)} %get-tuple-element.37.refs_1_.refs_3_, ...), custom_call_target="tpu_custom_call" | custom-call | flops 8053063680 | bytes 17825792 | tf_op jit(solution)/shard_map/pallas_call | solution.py:144
  160.8 2.3 %all-to-all-done.3 = f32[16,1,16,1536]{3,2,1,0:T(8,128)S(1)} async-done(((f32[16,1,16,1536]{3,2,1,0:T(8,128)}), f32[16,1,16,1536]{3,2,1,0:T(8,128)S(1)}, u32[]{:S(2)}, u32[]{:S(2)}) %all-to-all-start.3) | async-done | bytes 1572896 | tf_op jit(solution)/shard_map/all_to_all | solution.py:177
  164.3 4.6 %all-to-all-start.4 = ((f32[16,2,16,1024]{3,2,1,0:T(8,128)}), f32[16,2,16,1024]{3,2,1,0:T(8,128)S(1)}, u32[]{:S(2)}, u32[]{:S(2)}) async-start(f32[16,2,16,1024]{3,2,1,0:T(8,128)} %shard_map.51), calls=%async_computation.4 | async-start | bytes 4194304 | tf_op jit(solution)/shard_map/all_to_all | solution.py:177
  171.9 28.2 %all-to-all-done.4 = f32[16,2,16,1024]{3,2,1,0:T(8,128)S(1)} async-done(((f32[16,2,16,1024]{3,2,1,0:T(8,128)}), f32[16,2,16,1024]{3,2,1,0:T(8,128)S(1)}, u32[]{:S(2)}, u32[]{:S(2)}) %all-to-all-start.4) | async-done | bytes 2097184 | tf_op jit(solution)/shard_map/all_to_all | solution.py:177
  (76 shorter events, 28.4 us)
Async XLA Ops:
  3.0 47.3 %collective-permute-start = (f32[20,16,1536]{2,1,0:T(8,128)}, f32[20,16,1536]{2,1,0:T(8,128)}, u32[]{:S(2)}, u32[]{:S(2)}) collective-permute-start(f32[20,16,1536]{2,1,0:T(8,128)} %slice.25), channel_id=1, source_target_pairs={{0,32},{16,48},{32,64},{48,80},{64,96},{80,112},{96,0},{112,16},{1... | collective-permute-start | bytes 5898248 | tf_op jit(solution)/shard_map/ppermute | solution.py:180
  5.0 45.3 %collective-permute-start.1 = (f32[20,16,1536]{2,1,0:T(8,128)}, f32[20,16,1536]{2,1,0:T(8,128)}, u32[]{:S(2)}, u32[]{:S(2)}) collective-permute-start(f32[20,16,1536]{2,1,0:T(8,128)} %slice.25), channel_id=1, source_target_pairs={{0,96},{16,112},{32,0},{48,16},{64,32},{80,48},{96,64},{112,80},{1... | collective-permute-start | bytes 5898248 | tf_op jit(solution)/shard_map/ppermute | solution.py:180
  14.1 44.5 %all-to-all-start = ((f32[16,16,2560]{2,1,0:T(8,128)}), f32[16,16,2560]{2,1,0:T(8,128)S(1)}, u32[]{:S(2)}, u32[]{:S(2)}) async-start(f32[16,16,2560]{2,1,0:T(8,128)} %shard_map.47), calls=%async_computation | async-start | bytes 5242880 | tf_op jit(solution)/shard_map/all_to_all | solution.py:177
  21.2 29.6 %copy-start.3 = (s32[1500]{0:T(1024)S(1)}, s32[1500]{0:T(1024)}, u32[]{:S(2)}) copy-start(s32[1500]{0:T(1024)} %param.7) | copy-start | bytes 18004
  21.2 54.5 %collective-permute-start.4 = (f32[20,16,1536]{2,1,0:T(8,128)}, f32[20,16,1536]{2,1,0:T(8,128)}, u32[]{:S(2)}, u32[]{:S(2)}) collective-permute-start(f32[20,16,1536]{2,1,0:T(8,128)} %slice.25), channel_id=1, source_target_pairs={{0,16},{16,0},{32,48},{48,32},{64,80},{80,64},{96,112},{112,96},{1... | collective-permute-start | bytes 5898248 | tf_op jit(solution)/shard_map/ppermute | solution.py:186
  50.3 30.3 %collective-permute-start.5 = (f32[20,16,1536]{2,1,0:T(8,128)}, f32[20,16,1536]{2,1,0:T(8,128)}, u32[]{:S(2)}, u32[]{:S(2)}) collective-permute-start(f32[20,16,1536]{2,1,0:T(8,128)} %collective-permute-done), channel_id=1, source_target_pairs={{0,16},{16,0},{32,48},{48,32},{64,80},{80,64},{96,112},{112,96},{1... | collective-permute-start | bytes 5898248 | tf_op jit(solution)/shard_map/ppermute | solution.py:186
  50.3 30.3 %collective-permute-start.6 = (f32[20,16,1536]{2,1,0:T(8,128)}, f32[20,16,1536]{2,1,0:T(8,128)}, u32[]{:S(2)}, u32[]{:S(2)}) collective-permute-start(f32[20,16,1536]{2,1,0:T(8,128)} %collective-permute-done.1), channel_id=1, source_target_pairs={{0,16},{16,0},{32,48},{48,32},{64,80},{80,64},{96,112},{112,96},{1... | collective-permute-start | bytes 5898248 | tf_op jit(solution)/shard_map/ppermute | solution.py:186
  55.4 25.2 %collective-permute-start.2 = (f32[10,16,1536]{2,1,0:T(8,128)}, f32[10,16,1536]{2,1,0:T(8,128)}, u32[]{:S(2)}, u32[]{:S(2)}) collective-permute-start(f32[10,16,1536]{2,1,0:T(8,128)} %slice.28), channel_id=1, source_target_pairs={{0,32},{16,48},{32,64},{48,80},{64,96},{80,112},{96,0},{112,16},{1... | collective-permute-start | bytes 2949128 | tf_op jit(solution)/shard_map/ppermute | solution.py:183
  56.6 23.9 %collective-permute-start.3 = (f32[10,16,1536]{2,1,0:T(8,128)}, f32[10,16,1536]{2,1,0:T(8,128)}, u32[]{:S(2)}, u32[]{:S(2)}) collective-permute-start(f32[10,16,1536]{2,1,0:T(8,128)} %slice.29), channel_id=1, source_target_pairs={{0,96},{16,112},{32,0},{48,16},{64,32},{80,48},{96,64},{112,80},{1... | collective-permute-start | bytes 2949128 | tf_op jit(solution)/shard_map/ppermute | solution.py:183
  60.2 43.3 %all-to-all-start.1 = ((f32[16,16,2560]{2,1,0:T(8,128)}), f32[16,16,2560]{2,1,0:T(8,128)S(1)}, u32[]{:S(2)}, u32[]{:S(2)}) async-start(f32[16,16,2560]{2,1,0:T(8,128)} %shard_map.46), calls=%async_computation.1 | async-start | bytes 5242880 | tf_op jit(solution)/shard_map/all_to_all | solution.py:177
  80.6 3.8 %collective-permute-start.9 = (f32[10,16,1536]{2,1,0:T(8,128)}, f32[10,16,1536]{2,1,0:T(8,128)S(1)}, u32[]{:S(2)}, u32[]{:S(2)}) collective-permute-start(f32[10,16,1536]{2,1,0:T(8,128)} %collective-permute-done.2), channel_id=1, source_target_pairs={{0,16},{16,0},{32,48},{48,32},{64,80},{80,64},{96,112},{112,96},{1... | collective-permute-start | bytes 2949128 | tf_op jit(solution)/shard_map/ppermute | solution.py:186
  80.7 4.2 %collective-permute-start.10 = (f32[10,16,1536]{2,1,0:T(8,128)}, f32[10,16,1536]{2,1,0:T(8,128)S(1)}, u32[]{:S(2)}, u32[]{:S(2)}) collective-permute-start(f32[10,16,1536]{2,1,0:T(8,128)} %collective-permute-done.3), channel_id=1, source_target_pairs={{0,16},{16,0},{32,48},{48,32},{64,80},{80,64},{96,112},{112,96},{1... | collective-permute-start | bytes 2949128 | tf_op jit(solution)/shard_map/ppermute | solution.py:186
  81.2 43.3 %collective-permute-start.7 = (f32[20,16,1024]{2,1,0:T(8,128)}, f32[20,16,1024]{2,1,0:T(8,128)}, u32[]{:S(2)}, u32[]{:S(2)}) collective-permute-start(f32[20,16,1024]{2,1,0:T(8,128)} %slice.27), channel_id=1, source_target_pairs={{0,32},{16,48},{32,64},{48,80},{64,96},{80,112},{96,0},{112,16},{1... | collective-permute-start | bytes 3932168 | tf_op jit(solution)/shard_map/ppermute | solution.py:180
  82.5 42.0 %collective-permute-start.8 = (f32[20,16,1024]{2,1,0:T(8,128)}, f32[20,16,1024]{2,1,0:T(8,128)}, u32[]{:S(2)}, u32[]{:S(2)}) collective-permute-start(f32[20,16,1024]{2,1,0:T(8,128)} %slice.27), channel_id=1, source_target_pairs={{0,96},{16,112},{32,0},{48,16},{64,32},{80,48},{96,64},{112,80},{1... | collective-permute-start | bytes 3932168 | tf_op jit(solution)/shard_map/ppermute | solution.py:180
  103.5 27.2 %all-to-all-start.2 = ((f32[16,1,16,1536]{3,2,1,0:T(8,128)}), f32[16,1,16,1536]{3,2,1,0:T(8,128)}, u32[]{:S(2)}, u32[]{:S(2)}) async-start(f32[16,1,16,1536]{3,2,1,0:T(8,128)} %shard_map.52), calls=%async_computation.2 | async-start | bytes 3145728 | tf_op jit(solution)/shard_map/all_to_all | solution.py:177
  125.6 15.8 %collective-permute-start.11 = (f32[10,16,1024]{2,1,0:T(8,128)S(1)}, f32[10,16,1024]{2,1,0:T(8,128)S(1)}, u32[]{:S(2)}, u32[]{:S(2)}) collective-permute-start(f32[10,16,1024]{2,1,0:T(8,128)S(1)} %slice.30), channel_id=1, source_target_pairs={{0,32},{16,48},{32,64},{48,80},{64,96},{80,112},{96,0},{112,16},{1... | collective-permute-start | bytes 1966088 | tf_op jit(solution)/shard_map/ppermute | solution.py:183
  126.9 15.7 %collective-permute-start.12 = (f32[10,16,1024]{2,1,0:T(8,128)S(1)}, f32[10,16,1024]{2,1,0:T(8,128)}, u32[]{:S(2)}, u32[]{:S(2)}) collective-permute-start(f32[10,16,1024]{2,1,0:T(8,128)S(1)} %slice.31), channel_id=1, source_target_pairs={{0,96},{16,112},{32,0},{48,16},{64,32},{80,48},{96,64},{112,80},{1... | collective-permute-start | bytes 1966088 | tf_op jit(solution)/shard_map/ppermute | solution.py:183
  130.2 12.9 %collective-permute-start.13 = (f32[20,16,1024]{2,1,0:T(8,128)}, f32[20,16,1024]{2,1,0:T(8,128)}, u32[]{:S(2)}, u32[]{:S(2)}) collective-permute-start(f32[20,16,1024]{2,1,0:T(8,128)} %slice.27), channel_id=1, source_target_pairs={{0,16},{16,0},{32,48},{48,32},{64,80},{80,64},{96,112},{112,96},{1... | collective-permute-start | bytes 3932168 | tf_op jit(solution)/shard_map/ppermute | solution.py:186
  130.2 12.9 %collective-permute-start.14 = (f32[20,16,1024]{2,1,0:T(8,128)}, f32[20,16,1024]{2,1,0:T(8,128)}, u32[]{:S(2)}, u32[]{:S(2)}) collective-permute-start(f32[20,16,1024]{2,1,0:T(8,128)} %collective-permute-done.7), channel_id=1, source_target_pairs={{0,16},{16,0},{32,48},{48,32},{64,80},{80,64},{96,112},{112,96},{1... | collective-permute-start | bytes 3932168 | tf_op jit(solution)/shard_map/ppermute | solution.py:186
  130.7 12.4 %collective-permute-start.15 = (f32[20,16,1024]{2,1,0:T(8,128)}, f32[20,16,1024]{2,1,0:T(8,128)}, u32[]{:S(2)}, u32[]{:S(2)}) collective-permute-start(f32[20,16,1024]{2,1,0:T(8,128)} %collective-permute-done.8), channel_id=1, source_target_pairs={{0,16},{16,0},{32,48},{48,32},{64,80},{80,64},{96,112},{112,96},{1... | collective-permute-start | bytes 3932168 | tf_op jit(solution)/shard_map/ppermute | solution.py:186
  130.7 32.4 %all-to-all-start.3 = ((f32[16,1,16,1536]{3,2,1,0:T(8,128)}), f32[16,1,16,1536]{3,2,1,0:T(8,128)S(1)}, u32[]{:S(2)}, u32[]{:S(2)}) async-start(f32[16,1,16,1536]{3,2,1,0:T(8,128)} %shard_map.50), calls=%async_computation.3 | async-start | bytes 3145728 | tf_op jit(solution)/shard_map/all_to_all | solution.py:177
  142.6 3.0 %collective-permute-start.16 = (f32[10,16,1024]{2,1,0:T(8,128)S(1)}, f32[10,16,1024]{2,1,0:T(8,128)S(1)}, u32[]{:S(2)}, u32[]{:S(2)}) collective-permute-start(f32[10,16,1024]{2,1,0:T(8,128)S(1)} %collective-permute-done.11), channel_id=1, source_target_pairs={{0,16},{16,0},{32,48},{48,32},{64,80},{80,64},{96,112},{112,96},{1... | collective-permute-start | bytes 1966088 | tf_op jit(solution)/shard_map/ppermute | solution.py:186
  142.6 3.2 %collective-permute-start.17 = (f32[10,16,1024]{2,1,0:T(8,128)}, f32[10,16,1024]{2,1,0:T(8,128)S(1)}, u32[]{:S(2)}, u32[]{:S(2)}) collective-permute-start(f32[10,16,1024]{2,1,0:T(8,128)} %collective-permute-done.12), channel_id=1, source_target_pairs={{0,16},{16,0},{32,48},{48,32},{64,80},{80,64},{96,112},{112,96},{1... | collective-permute-start | bytes 1966088 | tf_op jit(solution)/shard_map/ppermute | solution.py:186
  164.3 35.8 %all-to-all-start.4 = ((f32[16,2,16,1024]{3,2,1,0:T(8,128)}), f32[16,2,16,1024]{3,2,1,0:T(8,128)S(1)}, u32[]{:S(2)}, u32[]{:S(2)}) async-start(f32[16,2,16,1024]{3,2,1,0:T(8,128)} %shard_map.51), calls=%async_computation.4 | async-start | bytes 4194304 | tf_op jit(solution)/shard_map/all_to_all | solution.py:177
  (9 other events, 27.0 us)

commit v4 on v3

--- a/solution.py
+++ b/solution.py
@@ -159,11 +159,34 @@
     )(order, *lefts, *panels)
 
 
+def halve_kernel(above_ref, below_ref, first_ref, second_ref):
+    first_ref[...] = above_ref[...]
+    second_ref[...] = below_ref[...]
+
+
+def halve(above, below):
+    slots, rows, width = above.shape
+    half, block = slots // 2, slots // 4
+    shape = jax.ShapeDtypeStruct((half, rows, width), above.dtype)
+    return pl.pallas_call(
+        halve_kernel,
+        grid=(half // block,),
+        in_specs=[
+            pl.BlockSpec((block, rows, width), lambda n: (n, 0, 0)),
+            pl.BlockSpec((block, rows, width), lambda n: (n + half // block, 0, 0)),
+        ],
+        out_specs=[pl.BlockSpec((block, rows, width), lambda n: (n, 0, 0))] * 2,
+        out_shape=[shape] * 2,
+        compiler_params=pltpu.CompilerParams(vmem_limit_bytes=56 * MIB),
+        cost_estimate=pl.CostEstimate(flops=0, bytes_accessed=16 * half * rows * width, transcendentals=0),
+    )(above, below)
+
+
 def body(amplitudes, integrals, occ_irrep, vir_irrep):
     rows, col = lax.axis_size("row"), lax.axis_size("col")
     wl, kt, al, ct = amplitudes.shape
     kl, cl, nt = integrals.shape
-    part, chips = kl // 2, rows // 2
+    chips = rows // 2
     cross = [(r, r ^ 1) for r in range(rows)]
     up = [(r, (r + 2) % rows) for r in range(rows)]
     down = [(r, (r - 2) % rows) for r in range(rows)]
@@ -180,7 +203,8 @@
         return [lax.ppermute(value, "row", up), lax.ppermute(value, "row", down)]
 
     def ring_on(near):
-        return [lax.ppermute(near[0][:part], "row", up), lax.ppermute(near[1][part:], "row", down)]
+        first, second = halve(*near)
+        return [lax.ppermute(first, "row", up), lax.ppermute(second, "row", down)]
 
     def other_core(values):
         return [lax.ppermute(value, "row", cross) for value in values]
@@ -198,8 +222,7 @@
     colmask = colmask.reshape(rows, kl * cl)
     colmask = jnp.concatenate([lax.dynamic_slice_in_dim(colmask, order[i], 1) for i in range(rows)], axis=1)
     left0 = to_rows(packed[0])
-    packed[1], left0 = lax.optimization_barrier((packed[1], left0))
-    left1 = to_rows(packed[1])
+    left1 = to_rows(lax.optimization_barrier((packed[1], left0))[0])
     halves = prepare(left0, colmask, row_sizes[0:1])
     (far0, over0) = lax.optimization_barrier((far0, over0, halves))[:2]
     (late, far0, over0) = lax.optimization_barrier((late, far0, over0))
@@ -209,9 +232,9 @@
     piece0 = multiply(order, halves, panels, al)
     moved0 = to_rows(lax.optimization_barrier((piece0, left1))[0])
     halves = halves + prepare(left1, colmask, row_sizes[1:2])
+    near1 = lax.optimization_barrier((near1, piece0, halves[2:]))[0]
+    far1 = ring_on(near1)
     piece1 = multiply(order, halves[2:], panels, al)
-    near1 = lax.optimization_barrier((near1, piece1))[0]
-    far1 = ring_on(near1)
     over1 = other_core([late, *near1])
     far1 = lax.optimization_barrier((far1, piece1))[0]
     over1 += other_core(far1)

time: 202 us -> 199 us (0.985)
  local copies, waits for them, and re-layouts: 19.2 us -> 12.3 us
  Pallas kernels: 60.1 us -> 64.7 us
    slice x4 -> x0, local copies, waits for them, and re-layouts: 6.7 us -> none  [the longest x2 3.35 us: ring_on(): near[1][part:]]
    pallas_call x0 -> x2, Pallas kernels: none -> 4.73 us  [halve(): pl.pallas_call(halve_kernel, grid=(half // block,), in_specs=[pl.BlockSpe...]
    ppermute x4, waiting for transfers between devices: 9.66 us -> 5.06 us  [ring_on(): return [lax.ppermute(first, 'row', up), lax.ppermute(second, 'row', down)]]
    all_to_all x5, waiting for transfers between devices: 35.1 us -> 38.5 us  [to_rows(): return lax.all_to_all(value, 'col', split_axis=0, concat_axis=0, tiled=True)]
    unnamed x20 -> x22, local copies, waits for them, and re-layouts: 4.59 us -> 4.43 us
  transfers between devices with their start and end apart: 23 -> 23, of which waited for: 10 -> 10; matrix products, arithmetic and copies ran while one was open for 8% -> 4% of each run, Pallas kernels for 30% -> 33%
where the time goes in v4:
time: 199 us; the launch traced here: 197 us
  waiting for transfers between devices  71.3 us (36%)
  Pallas kernels  64.7 us (33%)
  starting transfers between devices  44.4 us (22%)
  local copies, waits for them, and re-layouts  12.3 us (6%)
  other arithmetic  4.46 us (2%)
    pallas_call x3, Pallas kernels, multiply(): pl.pallas_call(functools.partial(multiply_kernel, panels=len(panels), lef...  40.1 us
    all_to_all x5, waiting for transfers between devices, to_rows(): return lax.all_to_all(value, 'col', split_axis=0, concat_axis=0, tiled=True)  38.5 us
    all_to_all x5, starting transfers between devices, to_rows(): return lax.all_to_all(value, 'col', split_axis=0, concat_axis=0, tiled=True)  28.3 us
    ppermute x4, waiting for transfers between devices, ring(): return [lax.ppermute(value, 'row', up), lax.ppermute(value, 'row', down)]  24.6 us
    pallas_call x2, Pallas kernels, pack(): pl.pallas_call(functools.partial(pack_kernel, width=width), grid_spec=plt...  12.7 us
    ppermute x4, starting transfers between devices, ring(): return [lax.ppermute(value, 'row', up), lax.ppermute(value, 'row', down)]  7.36 us
    pallas_call x2, Pallas kernels, prepare(): pl.pallas_call(prepare_kernel, grid_spec=pltpu.PrefetchScalarGridSpec(num...  7.2 us
    ppermute x4, starting transfers between devices, ring_on(): return [lax.ppermute(first, 'row', up), lax.ppermute(second, 'row', down)]  6.47 us
  transfers between devices with their start and end apart: 23, of which 10 were waited for; matrix products, arithmetic and copies ran while one was open for 4% of the time, Pallas kernels for 33%

profile of v4, /device:TPU:0, one launch (start us, length us, event | category | flops | bytes accessed | tf_op | source)
XLA Modules:
  0.0 197.4 jit_solution(16083094081367074997)
XLA Ops:
  0.0 3.0 %slice.14 = f32[20,16,1536]{2,1,0:T(8,128)} slice(f32[20,16,2560]{2,1,0:T(8,128)} %param.5), slice={[0:20], [0:16], [1024:2560]} | slice | bytes 3932160 | tf_op jit(solution)/shard_map/slice | solution.py:216
  3.0 2.0 %collective-permute-start = (f32[20,16,1536]{2,1,0:T(8,128)}, f32[20,16,1536]{2,1,0:T(8,128)}, u32[]{:S(2)}, u32[]{:S(2)}) collective-permute-start(f32[20,16,1536]{2,1,0:T(8,128)} %slice.14), channel_id=1, source_target_pairs={{0,32},{16,48},{32,64},{48,80},{64,96},{80,112},{96,0},{112,16},{1... | collective-permute-start | bytes 5898248 | tf_op jit(solution)/shard_map/ppermute | solution.py:203
  5.0 2.1 %collective-permute-start.1 = (f32[20,16,1536]{2,1,0:T(8,128)}, f32[20,16,1536]{2,1,0:T(8,128)}, u32[]{:S(2)}, u32[]{:S(2)}) collective-permute-start(f32[20,16,1536]{2,1,0:T(8,128)} %slice.14), channel_id=1, source_target_pairs={{0,96},{16,112},{32,0},{48,16},{64,32},{80,48},{96,64},{112,80},{1... | collective-permute-start | bytes 5898248 | tf_op jit(solution)/shard_map/ppermute | solution.py:203
  7.8 6.4 %shard_map.46 = f32[16,16,2560]{2,1,0:T(8,128)} custom-call(s32[8]{0:T(128)} %stack.35.order_ref.refs_0_, f32[2,160,16,256]{3,2,1,0:T(8,128)} %second_ref.3, f32[2,160,16,256]{3,2,1,0:T(8,128)} %second_ref.3), custom_call_target="tpu_custom_call" | custom-call | flops 655360 | bytes 5242880 | tf_op jit(solution)/shard_map/pallas_call | solution.py:68
  14.1 7.0 %all-to-all-start = ((f32[16,16,2560]{2,1,0:T(8,128)}), f32[16,16,2560]{2,1,0:T(8,128)S(1)}, u32[]{:S(2)}, u32[]{:S(2)}) async-start(f32[16,16,2560]{2,1,0:T(8,128)} %shard_map.46), calls=%async_computation | async-start | bytes 5242880 | tf_op jit(solution)/shard_map/all_to_all | solution.py:200
  21.3 6.4 %shard_map.48 = f32[16,16,2560]{2,1,0:T(8,128)} custom-call(s32[8]{0:T(128)} %stack.35.order_ref.refs_0_, f32[2,160,16,256]{3,2,1,0:T(8,128)} %second_ref.3, f32[2,160,16,256]{3,2,1,0:T(8,128)} %second_ref.3), custom_call_target="tpu_custom_call" | custom-call | flops 655360 | bytes 5242880 | tf_op jit(solution)/shard_map/pallas_call | solution.py:68
  27.6 22.6 %collective-permute-done.above_ref = f32[20,16,1536]{2,1,0:T(8,128)} collective-permute-done((f32[20,16,1536]{2,1,0:T(8,128)}, f32[20,16,1536]{2,1,0:T(8,128)}, u32[]{:S(2)}, u32[]{:S(2)}) %collective-permute-start) | collective-permute-done | bytes 1966112 | tf_op jit(solution)/shard_map/ppermute | solution.py:203
  50.9 2.5 %shard_map.50 = (f32[10,16,1536]{2,1,0:T(8,128)}, f32[10,16,1536]{2,1,0:T(8,128)}) custom-call(f32[20,16,1536]{2,1,0:T(8,128)} %collective-permute-done.above_ref, f32[20,16,1536]{2,1,0:T(8,128)} %collective-permute-done.1.below_ref), custom_call_target="tpu_custom_call" | custom-call | bytes 3932160 | tf_op jit(solution)/shard_map/pallas_call | solution.py:171
  54.7 2.0 %collective-permute-start.3 = (f32[10,16,1536]{2,1,0:T(8,128)}, f32[10,16,1536]{2,1,0:T(8,128)}, u32[]{:S(2)}, u32[]{:S(2)}) collective-permute-start(f32[10,16,1536]{2,1,0:T(8,128)} %get-tuple-element.44), channel_id=1, source_target_pairs={{0,96},{16,112},{32,0},{48,16},{64,32},{80,48},{96,64},{112,80},{1... | collective-permute-start | bytes 2949128 | tf_op jit(solution)/shard_map/ppermute | solution.py:207
  59.1 6.1 %all-to-all-start.1 = ((f32[16,16,2560]{2,1,0:T(8,128)}), f32[16,16,2560]{2,1,0:T(8,128)S(1)}, u32[]{:S(2)}, u32[]{:S(2)}) async-start(f32[16,16,2560]{2,1,0:T(8,128)} %shard_map.48), calls=%async_computation.1 | async-start | bytes 5242880 | tf_op jit(solution)/shard_map/all_to_all | solution.py:200
  65.3 2.5 %slice.15 = f32[20,16,1024]{2,1,0:T(8,128)} slice(f32[20,16,2560]{2,1,0:T(8,128)} %param.5), slice={[0:20], [0:16], [0:1024]} | slice | bytes 2621440 | tf_op jit(solution)/shard_map/slice | solution.py:216
  70.0 3.6 %shard_map.47 = (bf16[256,2560]{1,0:T(8,128)(2,1)}, bf16[256,2560]{1,0:T(8,128)(2,1)}) custom-call(s32[1]{0:T(128)} %get-tuple-element.73.size_ref, f32[256,2560]{1,0:T(8,128)} %bitcast.33, f32[1,2560]{1,0:T(1,128)} %concatenate.9.mask_ref), custom_call_target="tpu_custom_call" | custom-call | flops 2621440 | bytes 5242880 | tf_op jit(solution)/shard_map/pallas_call | solution.py:102
  73.6 5.1 %collective-permute-done.2 = f32[10,16,1536]{2,1,0:T(8,128)} collective-permute-done((f32[10,16,1536]{2,1,0:T(8,128)}, f32[10,16,1536]{2,1,0:T(8,128)}, u32[]{:S(2)}, u32[]{:S(2)}) %collective-permute-start.2) | collective-permute-done | bytes 983072 | tf_op jit(solution)/shard_map/ppermute | solution.py:207
  83.9 12.9 %shard_map.51 = f32[16,1,16,1536]{3,2,1,0:T(8,128)} custom-call(s32[8]{0:T(128)} %stack.35.order_ref.refs_0_, bf16[256,2560]{1,0:T(8,128)(2,1)} %get-tuple-element.35.refs_1_, bf16[256,2560]{1,0:T(8,128)(2,1)} %get-tuple-element.36.refs_2_, f32[320,1536]{1,0:T(8,128)} %bitcast.11.refs_3_, f32[320,1536]{1,0:T(8,128)} %bitcast.12.refs_4_, ...), custom_call_target="tpu_custom_call" | custom-call | flops 6039797760 | bytes 19922944 | tf_op jit(solution)/shard_map/pallas_call | solution.py:144
  96.8 4.8 %all-to-all-done.1 = f32[16,16,2560]{2,1,0:T(8,128)S(1)} async-done(((f32[16,16,2560]{2,1,0:T(8,128)}), f32[16,16,2560]{2,1,0:T(8,128)S(1)}, u32[]{:S(2)}, u32[]{:S(2)}) %all-to-all-start.1) | async-done | bytes 2621472 | tf_op jit(solution)/shard_map/all_to_all | solution.py:200
  101.6 4.4 %all-to-all-start.2 = ((f32[16,1,16,1536]{3,2,1,0:T(8,128)}), f32[16,1,16,1536]{3,2,1,0:T(8,128)}, u32[]{:S(2)}, u32[]{:S(2)}) async-start(f32[16,1,16,1536]{3,2,1,0:T(8,128)} %shard_map.51), calls=%async_computation.2 | async-start | bytes 3145728 | tf_op jit(solution)/shard_map/all_to_all | solution.py:200
  106.0 3.6 %shard_map.49 = (bf16[256,2560]{1,0:T(8,128)(2,1)}, bf16[256,2560]{1,0:T(8,128)(2,1)}) custom-call(s32[1]{0:T(128)} %get-tuple-element.74.size_ref, f32[256,2560]{1,0:T(8,128)} %bitcast.32, f32[1,2560]{1,0:T(1,128)} %concatenate.9.mask_ref), custom_call_target="tpu_custom_call" | custom-call | flops 2621440 | bytes 5242880 | tf_op jit(solution)/shard_map/pallas_call | solution.py:102
  111.6 2.2 %shard_map.52 = (f32[10,16,1024]{2,1,0:T(8,128)}, f32[10,16,1024]{2,1,0:T(8,128)}) custom-call(f32[20,16,1024]{2,1,0:T(8,128)} %collective-permute-done.7.above_ref, f32[20,16,1024]{2,1,0:T(8,128)} %collective-permute-done.8.below_ref), custom_call_target="tpu_custom_call" | custom-call | bytes 2621440 | tf_op jit(solution)/shard_map/pallas_call | solution.py:171
  117.5 13.0 %shard_map.53 = f32[16,1,16,1536]{3,2,1,0:T(8,128)} custom-call(s32[8]{0:T(128)} %stack.35.order_ref.refs_0_, bf16[256,2560]{1,0:T(8,128)(2,1)} %get-tuple-element.39.refs_1_.refs_3_, bf16[256,2560]{1,0:T(8,128)(2,1)} %get-tuple-element.40.refs_2_.refs_4_, f32[320,1536]{1,0:T(8,128)} %bitcast.11.refs_3_, f32[320,1536]{1,0:T(8,128)} %bitcast.12.refs_4_, ...), custom_call_target="tpu_custom_call" | custom-call | flops 6039797760 | bytes 19922944 | tf_op jit(solution)/shard_map/pallas_call | solution.py:144
  130.5 7.0 %all-to-all-start.3 = ((f32[16,1,16,1536]{3,2,1,0:T(8,128)}), f32[16,1,16,1536]{3,2,1,0:T(8,128)S(1)}, u32[]{:S(2)}, u32[]{:S(2)}) async-start(f32[16,1,16,1536]{3,2,1,0:T(8,128)} %shard_map.53), calls=%async_computation.3 | async-start | bytes 3145728 | tf_op jit(solution)/shard_map/all_to_all | solution.py:200
  141.7 14.2 %shard_map.54 = f32[16,2,16,1024]{3,2,1,0:T(8,128)} custom-call(s32[8]{0:T(128)} %stack.35.order_ref.refs_0_, bf16[256,2560]{1,0:T(8,128)(2,1)} %get-tuple-element.35.refs_1_, bf16[256,2560]{1,0:T(8,128)(2,1)} %get-tuple-element.36.refs_2_, bf16[256,2560]{1,0:T(8,128)(2,1)} %get-tuple-element.39.refs_1_.refs_3_, ...), custom_call_target="tpu_custom_call" | custom-call | flops 8053063680 | bytes 17825792 | tf_op jit(solution)/shard_map/pallas_call | solution.py:144
  155.9 6.9 %all-to-all-done.3 = f32[16,1,16,1536]{3,2,1,0:T(8,128)S(1)} async-done(((f32[16,1,16,1536]{3,2,1,0:T(8,128)}), f32[16,1,16,1536]{3,2,1,0:T(8,128)S(1)}, u32[]{:S(2)}, u32[]{:S(2)}) %all-to-all-start.3) | async-done | bytes 1572896 | tf_op jit(solution)/shard_map/all_to_all | solution.py:200
  164.0 3.7 %all-to-all-start.4 = ((f32[16,2,16,1024]{3,2,1,0:T(8,128)}), f32[16,2,16,1024]{3,2,1,0:T(8,128)S(1)}, u32[]{:S(2)}, u32[]{:S(2)}) async-start(f32[16,2,16,1024]{3,2,1,0:T(8,128)} %shard_map.54), calls=%async_computation.4 | async-start | bytes 4194304 | tf_op jit(solution)/shard_map/all_to_all | solution.py:200
  170.7 25.9 %all-to-all-done.4 = f32[16,2,16,1024]{3,2,1,0:T(8,128)S(1)} async-done(((f32[16,2,16,1024]{3,2,1,0:T(8,128)}), f32[16,2,16,1024]{3,2,1,0:T(8,128)S(1)}, u32[]{:S(2)}, u32[]{:S(2)}) %all-to-all-start.4) | async-done | bytes 2097184 | tf_op jit(solution)/shard_map/all_to_all | solution.py:200
  (76 shorter events, 27.2 us)
Async XLA Ops:
  3.0 47.3 %collective-permute-start = (f32[20,16,1536]{2,1,0:T(8,128)}, f32[20,16,1536]{2,1,0:T(8,128)}, u32[]{:S(2)}, u32[]{:S(2)}) collective-permute-start(f32[20,16,1536]{2,1,0:T(8,128)} %slice.14), channel_id=1, source_target_pairs={{0,32},{16,48},{32,64},{48,80},{64,96},{80,112},{96,0},{112,16},{1... | collective-permute-start | bytes 5898248 | tf_op jit(solution)/shard_map/ppermute | solution.py:203
  5.0 45.3 %collective-permute-start.1 = (f32[20,16,1536]{2,1,0:T(8,128)}, f32[20,16,1536]{2,1,0:T(8,128)}, u32[]{:S(2)}, u32[]{:S(2)}) collective-permute-start(f32[20,16,1536]{2,1,0:T(8,128)} %slice.14), channel_id=1, source_target_pairs={{0,96},{16,112},{32,0},{48,16},{64,32},{80,48},{96,64},{112,80},{1... | collective-permute-start | bytes 5898248 | tf_op jit(solution)/shard_map/ppermute | solution.py:203
  14.1 43.5 %all-to-all-start = ((f32[16,16,2560]{2,1,0:T(8,128)}), f32[16,16,2560]{2,1,0:T(8,128)S(1)}, u32[]{:S(2)}, u32[]{:S(2)}) async-start(f32[16,16,2560]{2,1,0:T(8,128)} %shard_map.46), calls=%async_computation | async-start | bytes 5242880 | tf_op jit(solution)/shard_map/all_to_all | solution.py:200
  21.2 29.6 %copy-start.3 = (s32[1500]{0:T(1024)S(1)}, s32[1500]{0:T(1024)}, u32[]{:S(2)}) copy-start(s32[1500]{0:T(1024)} %param.7) | copy-start | bytes 18004
  21.2 52.4 %collective-permute-start.4 = (f32[20,16,1536]{2,1,0:T(8,128)}, f32[20,16,1536]{2,1,0:T(8,128)}, u32[]{:S(2)}, u32[]{:S(2)}) collective-permute-start(f32[20,16,1536]{2,1,0:T(8,128)} %slice.14), channel_id=1, source_target_pairs={{0,16},{16,0},{32,48},{48,32},{64,80},{80,64},{96,112},{112,96},{1... | collective-permute-start | bytes 5898248 | tf_op jit(solution)/shard_map/ppermute | solution.py:210
  50.3 28.4 %collective-permute-start.5 = (f32[20,16,1536]{2,1,0:T(8,128)}, f32[20,16,1536]{2,1,0:T(8,128)}, u32[]{:S(2)}, u32[]{:S(2)}) collective-permute-start(f32[20,16,1536]{2,1,0:T(8,128)} %collective-permute-done.above_ref), channel_id=1, source_target_pairs={{0,16},{16,0},{32,48},{48,32},{64,80},{80,64},{96,112},{112,96},{1... | collective-permute-start | bytes 5898248 | tf_op jit(solution)/shard_map/ppermute | solution.py:210
  50.3 28.4 %collective-permute-start.6 = (f32[20,16,1536]{2,1,0:T(8,128)}, f32[20,16,1536]{2,1,0:T(8,128)}, u32[]{:S(2)}, u32[]{:S(2)}) collective-permute-start(f32[20,16,1536]{2,1,0:T(8,128)} %collective-permute-done.1.below_ref), channel_id=1, source_target_pairs={{0,16},{16,0},{32,48},{48,32},{64,80},{80,64},{96,112},{112,96},{1... | collective-permute-start | bytes 5898248 | tf_op jit(solution)/shard_map/ppermute | solution.py:210
  53.5 25.2 %collective-permute-start.2 = (f32[10,16,1536]{2,1,0:T(8,128)}, f32[10,16,1536]{2,1,0:T(8,128)}, u32[]{:S(2)}, u32[]{:S(2)}) collective-permute-start(f32[10,16,1536]{2,1,0:T(8,128)} %get-tuple-element.43), channel_id=1, source_target_pairs={{0,32},{16,48},{32,64},{48,80},{64,96},{80,112},{96,0},{112,16},{1... | collective-permute-start | bytes 2949128 | tf_op jit(solution)/shard_map/ppermute | solution.py:207
  54.7 23.9 %collective-permute-start.3 = (f32[10,16,1536]{2,1,0:T(8,128)}, f32[10,16,1536]{2,1,0:T(8,128)}, u32[]{:S(2)}, u32[]{:S(2)}) collective-permute-start(f32[10,16,1536]{2,1,0:T(8,128)} %get-tuple-element.44), channel_id=1, source_target_pairs={{0,96},{16,112},{32,0},{48,16},{64,32},{80,48},{96,64},{112,80},{1... | collective-permute-start | bytes 2949128 | tf_op jit(solution)/shard_map/ppermute | solution.py:207
  59.1 42.5 %all-to-all-start.1 = ((f32[16,16,2560]{2,1,0:T(8,128)}), f32[16,16,2560]{2,1,0:T(8,128)S(1)}, u32[]{:S(2)}, u32[]{:S(2)}) async-start(f32[16,16,2560]{2,1,0:T(8,128)} %shard_map.48), calls=%async_computation.1 | async-start | bytes 5242880 | tf_op jit(solution)/shard_map/all_to_all | solution.py:200
  78.7 3.8 %collective-permute-start.9 = (f32[10,16,1536]{2,1,0:T(8,128)}, f32[10,16,1536]{2,1,0:T(8,128)S(1)}, u32[]{:S(2)}, u32[]{:S(2)}) collective-permute-start(f32[10,16,1536]{2,1,0:T(8,128)} %collective-permute-done.2), channel_id=1, source_target_pairs={{0,16},{16,0},{32,48},{48,32},{64,80},{80,64},{96,112},{112,96},{1... | collective-permute-start | bytes 2949128 | tf_op jit(solution)/shard_map/ppermute | solution.py:210
  78.8 4.2 %collective-permute-start.10 = (f32[10,16,1536]{2,1,0:T(8,128)}, f32[10,16,1536]{2,1,0:T(8,128)S(1)}, u32[]{:S(2)}, u32[]{:S(2)}) collective-permute-start(f32[10,16,1536]{2,1,0:T(8,128)} %collective-permute-done.3), channel_id=1, source_target_pairs={{0,16},{16,0},{32,48},{48,32},{64,80},{80,64},{96,112},{112,96},{1... | collective-permute-start | bytes 2949128 | tf_op jit(solution)/shard_map/ppermute | solution.py:210
  79.3 32.3 %collective-permute-start.7 = (f32[20,16,1024]{2,1,0:T(8,128)}, f32[20,16,1024]{2,1,0:T(8,128)}, u32[]{:S(2)}, u32[]{:S(2)}) collective-permute-start(f32[20,16,1024]{2,1,0:T(8,128)} %slice.15), channel_id=1, source_target_pairs={{0,32},{16,48},{32,64},{48,80},{64,96},{80,112},{96,0},{112,16},{1... | collective-permute-start | bytes 3932168 | tf_op jit(solution)/shard_map/ppermute | solution.py:203
  80.6 31.0 %collective-permute-start.8 = (f32[20,16,1024]{2,1,0:T(8,128)}, f32[20,16,1024]{2,1,0:T(8,128)}, u32[]{:S(2)}, u32[]{:S(2)}) collective-permute-start(f32[20,16,1024]{2,1,0:T(8,128)} %slice.15), channel_id=1, source_target_pairs={{0,96},{16,112},{32,0},{48,16},{64,32},{80,48},{96,64},{112,80},{1... | collective-permute-start | bytes 3932168 | tf_op jit(solution)/shard_map/ppermute | solution.py:203
  101.6 28.9 %all-to-all-start.2 = ((f32[16,1,16,1536]{3,2,1,0:T(8,128)}), f32[16,1,16,1536]{3,2,1,0:T(8,128)}, u32[]{:S(2)}, u32[]{:S(2)}) async-start(f32[16,1,16,1536]{3,2,1,0:T(8,128)} %shard_map.51), calls=%async_computation.2 | async-start | bytes 3145728 | tf_op jit(solution)/shard_map/all_to_all | solution.py:200
  113.8 23.8 %collective-permute-start.11 = (f32[10,16,1024]{2,1,0:T(8,128)}, f32[10,16,1024]{2,1,0:T(8,128)S(1)}, u32[]{:S(2)}, u32[]{:S(2)}) collective-permute-start(f32[10,16,1024]{2,1,0:T(8,128)} %get-tuple-element.58), channel_id=1, source_target_pairs={{0,32},{16,48},{32,64},{48,80},{64,96},{80,112},{96,0},{112,16},{1... | collective-permute-start | bytes 1966088 | tf_op jit(solution)/shard_map/ppermute | solution.py:207
  115.1 22.5 %collective-permute-start.12 = (f32[10,16,1024]{2,1,0:T(8,128)}, f32[10,16,1024]{2,1,0:T(8,128)}, u32[]{:S(2)}, u32[]{:S(2)}) collective-permute-start(f32[10,16,1024]{2,1,0:T(8,128)} %get-tuple-element.59), channel_id=1, source_target_pairs={{0,96},{16,112},{32,0},{48,16},{64,32},{80,48},{96,64},{112,80},{1... | collective-permute-start | bytes 1966088 | tf_op jit(solution)/shard_map/ppermute | solution.py:207
  117.0 21.2 %collective-permute-start.13 = (f32[20,16,1024]{2,1,0:T(8,128)}, f32[20,16,1024]{2,1,0:T(8,128)S(1)}, u32[]{:S(2)}, u32[]{:S(2)}) collective-permute-start(f32[20,16,1024]{2,1,0:T(8,128)} %slice.15), channel_id=1, source_target_pairs={{0,16},{16,0},{32,48},{48,32},{64,80},{80,64},{96,112},{112,96},{1... | collective-permute-start | bytes 3932168 | tf_op jit(solution)/shard_map/ppermute | solution.py:210
  117.0 21.2 %collective-permute-start.14 = (f32[20,16,1024]{2,1,0:T(8,128)}, f32[20,16,1024]{2,1,0:T(8,128)}, u32[]{:S(2)}, u32[]{:S(2)}) collective-permute-start(f32[20,16,1024]{2,1,0:T(8,128)} %collective-permute-done.7.above_ref), channel_id=1, source_target_pairs={{0,16},{16,0},{32,48},{48,32},{64,80},{80,64},{96,112},{112,96},{1... | collective-permute-start | bytes 3932168 | tf_op jit(solution)/shard_map/ppermute | solution.py:210
  117.5 20.7 %collective-permute-start.15 = (f32[20,16,1024]{2,1,0:T(8,128)}, f32[20,16,1024]{2,1,0:T(8,128)}, u32[]{:S(2)}, u32[]{:S(2)}) collective-permute-start(f32[20,16,1024]{2,1,0:T(8,128)} %collective-permute-done.8.below_ref), channel_id=1, source_target_pairs={{0,16},{16,0},{32,48},{48,32},{64,80},{80,64},{96,112},{112,96},{1... | collective-permute-start | bytes 3932168 | tf_op jit(solution)/shard_map/ppermute | solution.py:210
  130.5 32.4 %all-to-all-start.3 = ((f32[16,1,16,1536]{3,2,1,0:T(8,128)}), f32[16,1,16,1536]{3,2,1,0:T(8,128)S(1)}, u32[]{:S(2)}, u32[]{:S(2)}) async-start(f32[16,1,16,1536]{3,2,1,0:T(8,128)} %shard_map.53), calls=%async_computation.3 | async-start | bytes 3145728 | tf_op jit(solution)/shard_map/all_to_all | solution.py:200
  137.6 2.2 %collective-permute-start.16 = (f32[10,16,1024]{2,1,0:T(8,128)S(1)}, f32[10,16,1024]{2,1,0:T(8,128)S(1)}, u32[]{:S(2)}, u32[]{:S(2)}) collective-permute-start(f32[10,16,1024]{2,1,0:T(8,128)S(1)} %collective-permute-done.11), channel_id=1, source_target_pairs={{0,16},{16,0},{32,48},{48,32},{64,80},{80,64},{96,112},{112,96},{1... | collective-permute-start | bytes 1966088 | tf_op jit(solution)/shard_map/ppermute | solution.py:210
  137.9 3.0 %collective-permute-start.17 = (f32[10,16,1024]{2,1,0:T(8,128)}, f32[10,16,1024]{2,1,0:T(8,128)S(1)}, u32[]{:S(2)}, u32[]{:S(2)}) collective-permute-start(f32[10,16,1024]{2,1,0:T(8,128)} %collective-permute-done.12), channel_id=1, source_target_pairs={{0,16},{16,0},{32,48},{48,32},{64,80},{80,64},{96,112},{112,96},{1... | collective-permute-start | bytes 1966088 | tf_op jit(solution)/shard_map/ppermute | solution.py:210
  164.0 32.6 %all-to-all-start.4 = ((f32[16,2,16,1024]{3,2,1,0:T(8,128)}), f32[16,2,16,1024]{3,2,1,0:T(8,128)S(1)}, u32[]{:S(2)}, u32[]{:S(2)}) async-start(f32[16,2,16,1024]{3,2,1,0:T(8,128)} %shard_map.54), calls=%async_computation.4 | async-start | bytes 4194304 | tf_op jit(solution)/shard_map/all_to_all | solution.py:200
  (10 other events, 27.5 us)

commit v5 on v4

--- a/solution.py
+++ b/solution.py
@@ -159,6 +159,50 @@
     )(order, *lefts, *panels)
 
 
+def multiply_raw_kernel(size_ref, left_ref, mask_ref, *refs):
+    panel_refs, (out_ref, left_high, left_low) = refs[:-3], refs[-3:]
+    block = 64
+
+    @pl.when(pl.program_id(0) == 0)
+    def _():
+        for start in range(0, left_ref.shape[0], block):
+            at = slice(start, start + block)
+            row = start + lax.broadcasted_iota(jnp.int32, (block, 1), 0)
+            keep = (row < size_ref[0]).astype(jnp.float32)
+            left_high[at], left_low[at] = split(left_ref[at] * mask_ref[...] * keep)
+
+    high, low = split(jnp.concatenate([ref[...] for ref in panel_refs], axis=0))
+    dot = functools.partial(jnp.dot, preferred_element_type=jnp.float32)
+    total = dot(left_high[...], high) + (dot(left_high[...], low) + dot(left_low[...], high))
+    out_ref[:, 0] = total.reshape(out_ref.shape[0], *out_ref.shape[2:])
+
+
+def multiply_raw(left, colmask, size, panels):
+    col, al, depth = left.shape
+    rows, width = col * al, panels[0].shape[1]
+    return pl.pallas_call(
+        multiply_raw_kernel,
+        grid_spec=pltpu.PrefetchScalarGridSpec(
+            num_scalar_prefetch=1,
+            grid=(width // TILE,),
+            in_specs=[
+                pl.BlockSpec((rows, depth), lambda n, s: (0, 0)),
+                pl.BlockSpec((1, depth), lambda n, s: (0, 0)),
+            ]
+            + [pl.BlockSpec((panel.shape[0], TILE), lambda n, s: (0, n)) for panel in panels],
+            out_specs=pl.BlockSpec((col, 1, al, TILE), lambda n, s: (0, 0, 0, n)),
+            scratch_shapes=[pltpu.VMEM((rows, depth), jnp.bfloat16)] * 2,
+        ),
+        out_shape=jax.ShapeDtypeStruct((col, 1, al, width), jnp.float32),
+        compiler_params=pltpu.CompilerParams(vmem_limit_bytes=56 * MIB),
+        cost_estimate=pl.CostEstimate(
+            flops=6 * rows * depth * width,
+            bytes_accessed=4 * (rows * depth + depth * width + rows * width),
+            transcendentals=0,
+        ),
+    )(size, left.reshape(rows, depth), colmask, *panels)
+
+
 def halve_kernel(above_ref, below_ref, first_ref, second_ref):
     first_ref[...] = above_ref[...]
     second_ref[...] = below_ref[...]
@@ -231,10 +275,10 @@
     panels = flat(early, *near0, *far0, *over0)
     piece0 = multiply(order, halves, panels, al)
     moved0 = to_rows(lax.optimization_barrier((piece0, left1))[0])
-    halves = halves + prepare(left1, colmask, row_sizes[1:2])
-    near1 = lax.optimization_barrier((near1, piece0, halves[2:]))[0]
+    piece1 = multiply_raw(left1, colmask, row_sizes[1:2], panels)
+    halves = halves + prepare(lax.optimization_barrier((left1, piece1))[0], colmask, row_sizes[1:2])
+    near1 = lax.optimization_barrier((near1, piece1))[0]
     far1 = ring_on(near1)
-    piece1 = multiply(order, halves[2:], panels, al)
     over1 = other_core([late, *near1])
     far1 = lax.optimization_barrier((far1, piece1))[0]
     over1 += other_core(far1)

time: 199 us -> 198 us (level)
    pallas_call x0 -> x1, Pallas kernels: none -> 13.5 us  [multiply_raw(): pl.pallas_call(multiply_raw_kernel, grid_spec=pltpu.PrefetchScalarGridSpe...]
    pallas_call x3 -> x2, Pallas kernels: 40.1 us -> 27.1 us  [multiply(): pl.pallas_call(functools.partial(multiply_kernel, panels=len(panels), lef...]
    ppermute x4, waiting for transfers between devices: 5.06 us -> 10.1 us  [ring_on(): return [lax.ppermute(first, 'row', up), lax.ppermute(second, 'row', down)]]
    ppermute x10, waiting for transfers between devices: 3.16 us -> 0.45 us  [other_core(): return [lax.ppermute(value, 'row', cross) for value in values]]
    all_to_all x5, waiting for transfers between devices: 38.5 us -> 36.3 us  [to_rows(): return lax.all_to_all(value, 'col', split_axis=0, concat_axis=0, tiled=True)]
    ppermute x4, waiting for transfers between devices: 24.6 us -> 22.6 us  [ring(): return [lax.ppermute(value, 'row', up), lax.ppermute(value, 'row', down)]]
  transfers between devices with their start and end apart: 23 -> 23, of which waited for: 10 -> 9; matrix products, arithmetic and copies ran while one was open for 4% -> 4% of each run, Pallas kernels for 33% -> 33%
where the time goes in v5:
time: 198 us; the launch traced here: 197 us
  waiting for transfers between devices  69.4 us (35%)
  Pallas kernels  65.4 us (33%)
  starting transfers between devices  44.8 us (23%)
  local copies, waits for them, and re-layouts  12.9 us (7%)
  other arithmetic  4.46 us (2%)
    all_to_all x5, waiting for transfers between devices, to_rows(): return lax.all_to_all(value, 'col', split_axis=0, concat_axis=0, tiled=True)  36.3 us
    all_to_all x5, starting transfers between devices, to_rows(): return lax.all_to_all(value, 'col', split_axis=0, concat_axis=0, tiled=True)  28.8 us
    pallas_call x2, Pallas kernels, multiply(): pl.pallas_call(functools.partial(multiply_kernel, panels=len(panels), lef...  27.1 us
    ppermute x4, waiting for transfers between devices, ring(): return [lax.ppermute(value, 'row', up), lax.ppermute(value, 'row', down)]  22.6 us
    pallas_call x1, Pallas kernels, multiply_raw(): pl.pallas_call(multiply_raw_kernel, grid_spec=pltpu.PrefetchScalarGridSpe...  13.5 us
    pallas_call x2, Pallas kernels, pack(): pl.pallas_call(functools.partial(pack_kernel, width=width), grid_spec=plt...  12.8 us
    ppermute x4, waiting for transfers between devices, ring_on(): return [lax.ppermute(first, 'row', up), lax.ppermute(second, 'row', down)]  10.1 us
    ppermute x4, starting transfers between devices, ring(): return [lax.ppermute(value, 'row', up), lax.ppermute(value, 'row', down)]  7.36 us
  transfers between devices with their start and end apart: 23, of which 9 were waited for; matrix products, arithmetic and copies ran while one was open for 4% of the time, Pallas kernels for 33%

profile of v5, /device:TPU:0, one launch (start us, length us, event | category | flops | bytes accessed | tf_op | source)
XLA Modules:
  0.0 197.3 jit_solution(5266469666490945557)
XLA Ops:
  0.0 3.0 %slice.15 = f32[20,16,1536]{2,1,0:T(8,128)} slice(f32[20,16,2560]{2,1,0:T(8,128)} %param.5), slice={[0:20], [0:16], [1024:2560]} | slice | bytes 3932160 | tf_op jit(solution)/shard_map/slice | solution.py:260
  5.0 2.1 %collective-permute-start.1 = (f32[20,16,1536]{2,1,0:T(8,128)}, f32[20,16,1536]{2,1,0:T(8,128)}, u32[]{:S(2)}, u32[]{:S(2)}) collective-permute-start(f32[20,16,1536]{2,1,0:T(8,128)} %slice.15), channel_id=1, source_target_pairs={{0,96},{16,112},{32,0},{48,16},{64,32},{80,48},{96,64},{112,80},{1... | collective-permute-start | bytes 5898248 | tf_op jit(solution)/shard_map/ppermute | solution.py:247
  7.7 6.4 %shard_map.46 = f32[16,16,2560]{2,1,0:T(8,128)} custom-call(s32[8]{0:T(128)} %stack.35.order_ref.refs_0_, f32[2,160,16,256]{3,2,1,0:T(8,128)} %second_ref.3, f32[2,160,16,256]{3,2,1,0:T(8,128)} %second_ref.3), custom_call_target="tpu_custom_call" | custom-call | flops 655360 | bytes 5242880 | tf_op jit(solution)/shard_map/pallas_call | solution.py:68
  14.1 7.0 %all-to-all-start = ((f32[16,16,2560]{2,1,0:T(8,128)}), f32[16,16,2560]{2,1,0:T(8,128)S(1)}, u32[]{:S(2)}, u32[]{:S(2)}) async-start(f32[16,16,2560]{2,1,0:T(8,128)} %shard_map.46), calls=%async_computation | async-start | bytes 5242880 | tf_op jit(solution)/shard_map/all_to_all | solution.py:244
  21.2 6.5 %shard_map.48 = f32[16,16,2560]{2,1,0:T(8,128)} custom-call(s32[8]{0:T(128)} %stack.35.order_ref.refs_0_, f32[2,160,16,256]{3,2,1,0:T(8,128)} %second_ref.3, f32[2,160,16,256]{3,2,1,0:T(8,128)} %second_ref.3), custom_call_target="tpu_custom_call" | custom-call | flops 655360 | bytes 5242880 | tf_op jit(solution)/shard_map/pallas_call | solution.py:68
  27.7 22.5 %collective-permute-done.above_ref = f32[20,16,1536]{2,1,0:T(8,128)} collective-permute-done((f32[20,16,1536]{2,1,0:T(8,128)}, f32[20,16,1536]{2,1,0:T(8,128)}, u32[]{:S(2)}, u32[]{:S(2)}) %collective-permute-start) | collective-permute-done | bytes 1966112 | tf_op jit(solution)/shard_map/ppermute | solution.py:247
  50.9 2.6 %shard_map.49 = (f32[10,16,1536]{2,1,0:T(8,128)}, f32[10,16,1536]{2,1,0:T(8,128)}) custom-call(f32[20,16,1536]{2,1,0:T(8,128)} %collective-permute-done.above_ref, f32[20,16,1536]{2,1,0:T(8,128)} %collective-permute-done.1.below_ref), custom_call_target="tpu_custom_call" | custom-call | bytes 3932160 | tf_op jit(solution)/shard_map/pallas_call | solution.py:215
  59.1 6.1 %all-to-all-start.1 = ((f32[16,16,2560]{2,1,0:T(8,128)}), f32[16,16,2560]{2,1,0:T(8,128)S(1)}, u32[]{:S(2)}, u32[]{:S(2)}) async-start(f32[16,16,2560]{2,1,0:T(8,128)} %shard_map.48), calls=%async_computation.1 | async-start | bytes 5242880 | tf_op jit(solution)/shard_map/all_to_all | solution.py:244
  65.4 2.5 %slice.16 = f32[20,16,1024]{2,1,0:T(8,128)} slice(f32[20,16,2560]{2,1,0:T(8,128)} %param.5), slice={[0:20], [0:16], [0:1024]} | slice | bytes 2621440 | tf_op jit(solution)/shard_map/slice | solution.py:260
  70.0 3.6 %shard_map.47 = (bf16[256,2560]{1,0:T(8,128)(2,1)}, bf16[256,2560]{1,0:T(8,128)(2,1)}) custom-call(s32[1]{0:T(128)} %get-tuple-element.75.size_ref, f32[256,2560]{1,0:T(8,128)} %bitcast.35, f32[1,2560]{1,0:T(1,128)} %concatenate.9.mask_ref), custom_call_target="tpu_custom_call" | custom-call | flops 2621440 | bytes 5242880 | tf_op jit(solution)/shard_map/pallas_call | solution.py:102
  73.6 5.0 %collective-permute-done.2 = f32[10,16,1536]{2,1,0:T(8,128)} collective-permute-done((f32[10,16,1536]{2,1,0:T(8,128)}, f32[10,16,1536]{2,1,0:T(8,128)}, u32[]{:S(2)}, u32[]{:S(2)}) %collective-permute-start.2) | collective-permute-done | bytes 983072 | tf_op jit(solution)/shard_map/ppermute | solution.py:251
  83.9 13.0 %shard_map.54 = f32[16,1,16,1536]{3,2,1,0:T(8,128)} custom-call(s32[8]{0:T(128)} %stack.35.order_ref.refs_0_, bf16[256,2560]{1,0:T(8,128)(2,1)} %get-tuple-element.36.refs_1_, bf16[256,2560]{1,0:T(8,128)(2,1)} %get-tuple-element.37.refs_2_, f32[320,1536]{1,0:T(8,128)} %bitcast.10.refs_0_.refs_3_, f32[320,1536]{1,0:T(8,128)} %bitcast.11.refs_1_.refs_4_, ...), custom_call_target="tpu_custom_call" | custom-call | flops 6039797760 | bytes 19922944 | tf_op jit(solution)/shard_map/pallas_call | solution.py:144
  96.9 4.7 %all-to-all-done.1 = f32[16,16,2560]{2,1,0:T(8,128)S(1)} async-done(((f32[16,16,2560]{2,1,0:T(8,128)}), f32[16,16,2560]{2,1,0:T(8,128)S(1)}, u32[]{:S(2)}, u32[]{:S(2)}) %all-to-all-start.1) | async-done | bytes 2621472 | tf_op jit(solution)/shard_map/all_to_all | solution.py:244
  101.6 4.4 %all-to-all-start.2 = ((f32[16,1,16,1536]{3,2,1,0:T(8,128)}), f32[16,1,16,1536]{3,2,1,0:T(8,128)}, u32[]{:S(2)}, u32[]{:S(2)}) async-start(f32[16,1,16,1536]{3,2,1,0:T(8,128)} %shard_map.54), calls=%async_computation.2 | async-start | bytes 3145728 | tf_op jit(solution)/shard_map/all_to_all | solution.py:244
  106.0 13.5 %shard_map.50 = f32[16,1,16,1536]{3,2,1,0:T(8,128)} custom-call(s32[1]{0:T(128)} %get-tuple-element.76.size_ref, f32[256,2560]{1,0:T(8,128)} %bitcast.33, f32[1,2560]{1,0:T(1,128)} %concatenate.9.mask_ref, f32[320,1536]{1,0:T(8,128)} %bitcast.10.refs_0_.refs_3_, f32[320,1536]{1,0:T(8,128)} %bitcast.11.refs_1_.refs_4_, f32[320,1536]{1,0:T(8,128)} %bitcast.12.refs_2_.refs_5_, ...), custom_call_target="tpu_custom_call" | custom-call | flops 6039797760 | bytes 19922944 | tf_op jit(solution)/shard_map/pallas_call | solution.py:183
  119.6 2.2 %shard_map.52 = (f32[10,16,1024]{2,1,0:T(8,128)}, f32[10,16,1024]{2,1,0:T(8,128)}) custom-call(f32[20,16,1024]{2,1,0:T(8,128)} %collective-permute-done.9.above_ref, f32[20,16,1024]{2,1,0:T(8,128)} %collective-permute-done.10.below_ref), custom_call_target="tpu_custom_call" | custom-call | bytes 2621440 | tf_op jit(solution)/shard_map/pallas_call | solution.py:215
  121.7 3.2 %collective-permute-start.12 = (f32[10,16,1024]{2,1,0:T(8,128)}, f32[10,16,1024]{2,1,0:T(8,128)}, u32[]{:S(2)}, u32[]{:S(2)}) collective-permute-start(f32[10,16,1024]{2,1,0:T(8,128)} %get-tuple-element.61), channel_id=1, source_target_pairs={{0,96},{16,112},{32,0},{48,16},{64,32},{80,48},{96,64},{112,80},{1... | collective-permute-start | bytes 1966088 | tf_op jit(solution)/shard_map/ppermute | solution.py:251
  125.5 2.3 %all-to-all-done.2 = f32[16,1,16,1536]{3,2,1,0:T(8,128)} async-done(((f32[16,1,16,1536]{3,2,1,0:T(8,128)}), f32[16,1,16,1536]{3,2,1,0:T(8,128)}, u32[]{:S(2)}, u32[]{:S(2)}) %all-to-all-start.2) | async-done | bytes 1572896 | tf_op jit(solution)/shard_map/all_to_all | solution.py:244
  127.8 4.8 %all-to-all-start.3 = ((f32[16,1,16,1536]{3,2,1,0:T(8,128)}), f32[16,1,16,1536]{3,2,1,0:T(8,128)S(1)}, u32[]{:S(2)}, u32[]{:S(2)}) async-start(f32[16,1,16,1536]{3,2,1,0:T(8,128)} %shard_map.50), calls=%async_computation.3 | async-start | bytes 3145728 | tf_op jit(solution)/shard_map/all_to_all | solution.py:244
  132.6 5.0 %collective-permute-done.11 = f32[10,16,1024]{2,1,0:T(8,128)S(1)} collective-permute-done((f32[10,16,1024]{2,1,0:T(8,128)}, f32[10,16,1024]{2,1,0:T(8,128)S(1)}, u32[]{:S(2)}, u32[]{:S(2)}) %collective-permute-start.11) | collective-permute-done | bytes 655392 | tf_op jit(solution)/shard_map/ppermute | solution.py:251
  138.2 3.6 %shard_map.51 = (bf16[256,2560]{1,0:T(8,128)(2,1)}, bf16[256,2560]{1,0:T(8,128)(2,1)}) custom-call(s32[1]{0:T(128)} %get-tuple-element.76.size_ref, f32[256,2560]{1,0:T(8,128)} %bitcast.34, f32[1,2560]{1,0:T(1,128)} %concatenate.9.mask_ref), custom_call_target="tpu_custom_call" | custom-call | flops 2621440 | bytes 5242880 | tf_op jit(solution)/shard_map/pallas_call | solution.py:102
  143.3 14.1 %shard_map.53 = f32[16,2,16,1024]{3,2,1,0:T(8,128)} custom-call(s32[8]{0:T(128)} %stack.35.order_ref.refs_0_, bf16[256,2560]{1,0:T(8,128)(2,1)} %get-tuple-element.36.refs_1_, bf16[256,2560]{1,0:T(8,128)(2,1)} %get-tuple-element.37.refs_2_, bf16[256,2560]{1,0:T(8,128)(2,1)} %get-tuple-element.55.refs_3_, bf16[256,2560]{1,0:T(8,128)(2,1)} %get-tuple-element.56.refs_4_, ...), custom_call_target="tpu_custom_call" | custom-call | flops 8053063680 | bytes 17825792 | tf_op jit(solution)/shard_map/pallas_call | solution.py:144
  159.1 6.4 %all-to-all-start.4 = ((f32[16,2,16,1024]{3,2,1,0:T(8,128)}), f32[16,2,16,1024]{3,2,1,0:T(8,128)S(1)}, u32[]{:S(2)}, u32[]{:S(2)}) async-start(f32[16,2,16,1024]{3,2,1,0:T(8,128)} %shard_map.53), calls=%async_computation.4 | async-start | bytes 4194304 | tf_op jit(solution)/shard_map/all_to_all | solution.py:244
  168.5 27.9 %all-to-all-done.4 = f32[16,2,16,1024]{3,2,1,0:T(8,128)S(1)} async-done(((f32[16,2,16,1024]{3,2,1,0:T(8,128)}), f32[16,2,16,1024]{3,2,1,0:T(8,128)S(1)}, u32[]{:S(2)}, u32[]{:S(2)}) %all-to-all-start.4) | async-done | bytes 2097184 | tf_op jit(solution)/shard_map/all_to_all | solution.py:244
  (76 shorter events, 24.4 us)
Async XLA Ops:
  3.0 47.3 %collective-permute-start = (f32[20,16,1536]{2,1,0:T(8,128)}, f32[20,16,1536]{2,1,0:T(8,128)}, u32[]{:S(2)}, u32[]{:S(2)}) collective-permute-start(f32[20,16,1536]{2,1,0:T(8,128)} %slice.15), channel_id=1, source_target_pairs={{0,32},{16,48},{32,64},{48,80},{64,96},{80,112},{96,0},{112,16},{1... | collective-permute-start | bytes 5898248 | tf_op jit(solution)/shard_map/ppermute | solution.py:247
  5.0 45.3 %collective-permute-start.1 = (f32[20,16,1536]{2,1,0:T(8,128)}, f32[20,16,1536]{2,1,0:T(8,128)}, u32[]{:S(2)}, u32[]{:S(2)}) collective-permute-start(f32[20,16,1536]{2,1,0:T(8,128)} %slice.15), channel_id=1, source_target_pairs={{0,96},{16,112},{32,0},{48,16},{64,32},{80,48},{96,64},{112,80},{1... | collective-permute-start | bytes 5898248 | tf_op jit(solution)/shard_map/ppermute | solution.py:247
  14.1 43.5 %all-to-all-start = ((f32[16,16,2560]{2,1,0:T(8,128)}), f32[16,16,2560]{2,1,0:T(8,128)S(1)}, u32[]{:S(2)}, u32[]{:S(2)}) async-start(f32[16,16,2560]{2,1,0:T(8,128)} %shard_map.46), calls=%async_computation | async-start | bytes 5242880 | tf_op jit(solution)/shard_map/all_to_all | solution.py:244
  21.1 29.6 %copy-start.3 = (s32[1500]{0:T(1024)S(1)}, s32[1500]{0:T(1024)}, u32[]{:S(2)}) copy-start(s32[1500]{0:T(1024)} %param.7) | copy-start | bytes 18004
  21.1 52.5 %collective-permute-start.4 = (f32[20,16,1536]{2,1,0:T(8,128)}, f32[20,16,1536]{2,1,0:T(8,128)}, u32[]{:S(2)}, u32[]{:S(2)}) collective-permute-start(f32[20,16,1536]{2,1,0:T(8,128)} %slice.15), channel_id=1, source_target_pairs={{0,16},{16,0},{32,48},{48,32},{64,80},{80,64},{96,112},{112,96},{1... | collective-permute-start | bytes 5898248 | tf_op jit(solution)/shard_map/ppermute | solution.py:254
  50.2 28.4 %collective-permute-start.5 = (f32[20,16,1536]{2,1,0:T(8,128)}, f32[20,16,1536]{2,1,0:T(8,128)}, u32[]{:S(2)}, u32[]{:S(2)}) collective-permute-start(f32[20,16,1536]{2,1,0:T(8,128)} %collective-permute-done.above_ref), channel_id=1, source_target_pairs={{0,16},{16,0},{32,48},{48,32},{64,80},{80,64},{96,112},{112,96},{1... | collective-permute-start | bytes 5898248 | tf_op jit(solution)/shard_map/ppermute | solution.py:254
  50.2 28.4 %collective-permute-start.6 = (f32[20,16,1536]{2,1,0:T(8,128)}, f32[20,16,1536]{2,1,0:T(8,128)}, u32[]{:S(2)}, u32[]{:S(2)}) collective-permute-start(f32[20,16,1536]{2,1,0:T(8,128)} %collective-permute-done.1.below_ref), channel_id=1, source_target_pairs={{0,16},{16,0},{32,48},{48,32},{64,80},{80,64},{96,112},{112,96},{1... | collective-permute-start | bytes 5898248 | tf_op jit(solution)/shard_map/ppermute | solution.py:254
  53.5 25.2 %collective-permute-start.2 = (f32[10,16,1536]{2,1,0:T(8,128)}, f32[10,16,1536]{2,1,0:T(8,128)}, u32[]{:S(2)}, u32[]{:S(2)}) collective-permute-start(f32[10,16,1536]{2,1,0:T(8,128)} %get-tuple-element.42), channel_id=1, source_target_pairs={{0,32},{16,48},{32,64},{48,80},{64,96},{80,112},{96,0},{112,16},{1... | collective-permute-start | bytes 2949128 | tf_op jit(solution)/shard_map/ppermute | solution.py:251
  54.7 23.9 %collective-permute-start.3 = (f32[10,16,1536]{2,1,0:T(8,128)}, f32[10,16,1536]{2,1,0:T(8,128)}, u32[]{:S(2)}, u32[]{:S(2)}) collective-permute-start(f32[10,16,1536]{2,1,0:T(8,128)} %get-tuple-element.43), channel_id=1, source_target_pairs={{0,96},{16,112},{32,0},{48,16},{64,32},{80,48},{96,64},{112,80},{1... | collective-permute-start | bytes 2949128 | tf_op jit(solution)/shard_map/ppermute | solution.py:251
  59.1 42.5 %all-to-all-start.1 = ((f32[16,16,2560]{2,1,0:T(8,128)}), f32[16,16,2560]{2,1,0:T(8,128)S(1)}, u32[]{:S(2)}, u32[]{:S(2)}) async-start(f32[16,16,2560]{2,1,0:T(8,128)} %shard_map.48), calls=%async_computation.1 | async-start | bytes 5242880 | tf_op jit(solution)/shard_map/all_to_all | solution.py:244
  78.7 3.8 %collective-permute-start.7 = (f32[10,16,1536]{2,1,0:T(8,128)}, f32[10,16,1536]{2,1,0:T(8,128)S(1)}, u32[]{:S(2)}, u32[]{:S(2)}) collective-permute-start(f32[10,16,1536]{2,1,0:T(8,128)} %collective-permute-done.2), channel_id=1, source_target_pairs={{0,16},{16,0},{32,48},{48,32},{64,80},{80,64},{96,112},{112,96},{1... | collective-permute-start | bytes 2949128 | tf_op jit(solution)/shard_map/ppermute | solution.py:254
  78.8 4.2 %collective-permute-start.8 = (f32[10,16,1536]{2,1,0:T(8,128)}, f32[10,16,1536]{2,1,0:T(8,128)S(1)}, u32[]{:S(2)}, u32[]{:S(2)}) collective-permute-start(f32[10,16,1536]{2,1,0:T(8,128)} %collective-permute-done.3), channel_id=1, source_target_pairs={{0,16},{16,0},{32,48},{48,32},{64,80},{80,64},{96,112},{112,96},{1... | collective-permute-start | bytes 2949128 | tf_op jit(solution)/shard_map/ppermute | solution.py:254
  79.2 40.3 %collective-permute-start.9 = (f32[20,16,1024]{2,1,0:T(8,128)}, f32[20,16,1024]{2,1,0:T(8,128)}, u32[]{:S(2)}, u32[]{:S(2)}) collective-permute-start(f32[20,16,1024]{2,1,0:T(8,128)} %slice.16), channel_id=1, source_target_pairs={{0,32},{16,48},{32,64},{48,80},{64,96},{80,112},{96,0},{112,16},{1... | collective-permute-start | bytes 3932168 | tf_op jit(solution)/shard_map/ppermute | solution.py:247
  80.6 39.0 %collective-permute-start.10 = (f32[20,16,1024]{2,1,0:T(8,128)}, f32[20,16,1024]{2,1,0:T(8,128)}, u32[]{:S(2)}, u32[]{:S(2)}) collective-permute-start(f32[20,16,1024]{2,1,0:T(8,128)} %slice.16), channel_id=1, source_target_pairs={{0,96},{16,112},{32,0},{48,16},{64,32},{80,48},{96,64},{112,80},{1... | collective-permute-start | bytes 3932168 | tf_op jit(solution)/shard_map/ppermute | solution.py:247
  101.6 26.2 %all-to-all-start.2 = ((f32[16,1,16,1536]{3,2,1,0:T(8,128)}), f32[16,1,16,1536]{3,2,1,0:T(8,128)}, u32[]{:S(2)}, u32[]{:S(2)}) async-start(f32[16,1,16,1536]{3,2,1,0:T(8,128)} %shard_map.54), calls=%async_computation.2 | async-start | bytes 3145728 | tf_op jit(solution)/shard_map/all_to_all | solution.py:244
  121.7 15.9 %collective-permute-start.11 = (f32[10,16,1024]{2,1,0:T(8,128)}, f32[10,16,1024]{2,1,0:T(8,128)S(1)}, u32[]{:S(2)}, u32[]{:S(2)}) collective-permute-start(f32[10,16,1024]{2,1,0:T(8,128)} %get-tuple-element.60), channel_id=1, source_target_pairs={{0,32},{16,48},{32,64},{48,80},{64,96},{80,112},{96,0},{112,16},{1... | collective-permute-start | bytes 1966088 | tf_op jit(solution)/shard_map/ppermute | solution.py:251
  121.7 15.9 %collective-permute-start.12 = (f32[10,16,1024]{2,1,0:T(8,128)}, f32[10,16,1024]{2,1,0:T(8,128)}, u32[]{:S(2)}, u32[]{:S(2)}) collective-permute-start(f32[10,16,1024]{2,1,0:T(8,128)} %get-tuple-element.61), channel_id=1, source_target_pairs={{0,96},{16,112},{32,0},{48,16},{64,32},{80,48},{96,64},{112,80},{1... | collective-permute-start | bytes 1966088 | tf_op jit(solution)/shard_map/ppermute | solution.py:251
  125.0 16.8 %collective-permute-start.13 = (f32[20,16,1024]{2,1,0:T(8,128)}, f32[20,16,1024]{2,1,0:T(8,128)S(1)}, u32[]{:S(2)}, u32[]{:S(2)}) collective-permute-start(f32[20,16,1024]{2,1,0:T(8,128)} %slice.16), channel_id=1, source_target_pairs={{0,16},{16,0},{32,48},{48,32},{64,80},{80,64},{96,112},{112,96},{1... | collective-permute-start | bytes 3932168 | tf_op jit(solution)/shard_map/ppermute | solution.py:254
  125.0 16.8 %collective-permute-start.14 = (f32[20,16,1024]{2,1,0:T(8,128)}, f32[20,16,1024]{2,1,0:T(8,128)}, u32[]{:S(2)}, u32[]{:S(2)}) collective-permute-start(f32[20,16,1024]{2,1,0:T(8,128)} %collective-permute-done.9.above_ref), channel_id=1, source_target_pairs={{0,16},{16,0},{32,48},{48,32},{64,80},{80,64},{96,112},{112,96},{1... | collective-permute-start | bytes 3932168 | tf_op jit(solution)/shard_map/ppermute | solution.py:254
  125.5 16.3 %collective-permute-start.15 = (f32[20,16,1024]{2,1,0:T(8,128)}, f32[20,16,1024]{2,1,0:T(8,128)}, u32[]{:S(2)}, u32[]{:S(2)}) collective-permute-start(f32[20,16,1024]{2,1,0:T(8,128)} %collective-permute-done.10.below_ref), channel_id=1, source_target_pairs={{0,16},{16,0},{32,48},{48,32},{64,80},{80,64},{96,112},{112,96},{1... | collective-permute-start | bytes 3932168 | tf_op jit(solution)/shard_map/ppermute | solution.py:254
  127.8 30.1 %all-to-all-start.3 = ((f32[16,1,16,1536]{3,2,1,0:T(8,128)}), f32[16,1,16,1536]{3,2,1,0:T(8,128)S(1)}, u32[]{:S(2)}, u32[]{:S(2)}) async-start(f32[16,1,16,1536]{3,2,1,0:T(8,128)} %shard_map.50), calls=%async_computation.3 | async-start | bytes 3145728 | tf_op jit(solution)/shard_map/all_to_all | solution.py:244
  137.6 4.1 %collective-permute-start.16 = (f32[10,16,1024]{2,1,0:T(8,128)S(1)}, f32[10,16,1024]{2,1,0:T(8,128)S(1)}, u32[]{:S(2)}, u32[]{:S(2)}) collective-permute-start(f32[10,16,1024]{2,1,0:T(8,128)S(1)} %collective-permute-done.11), channel_id=1, source_target_pairs={{0,16},{16,0},{32,48},{48,32},{64,80},{80,64},{96,112},{112,96},{1... | collective-permute-start | bytes 1966088 | tf_op jit(solution)/shard_map/ppermute | solution.py:254
  137.6 4.2 %collective-permute-start.17 = (f32[10,16,1024]{2,1,0:T(8,128)}, f32[10,16,1024]{2,1,0:T(8,128)S(1)}, u32[]{:S(2)}, u32[]{:S(2)}) collective-permute-start(f32[10,16,1024]{2,1,0:T(8,128)} %collective-permute-done.12), channel_id=1, source_target_pairs={{0,16},{16,0},{32,48},{48,32},{64,80},{80,64},{96,112},{112,96},{1... | collective-permute-start | bytes 1966088 | tf_op jit(solution)/shard_map/ppermute | solution.py:254
  159.1 37.3 %all-to-all-start.4 = ((f32[16,2,16,1024]{3,2,1,0:T(8,128)}), f32[16,2,16,1024]{3,2,1,0:T(8,128)S(1)}, u32[]{:S(2)}, u32[]{:S(2)}) async-start(f32[16,2,16,1024]{3,2,1,0:T(8,128)} %shard_map.53), calls=%async_computation.4 | async-start | bytes 4194304 | tf_op jit(solution)/shard_map/all_to_all | solution.py:244
  (10 other events, 27.5 us)
